TPU v7x, 32 devices: a whole 2x2x4 slice. The times are simulated.
32 devices in a mesh: groups: 2 (over x), lat: 16 (over z, y, core).
Axes of the slice: x: 2, y: 2, z: 4, core: 2. Of those that a mesh axis runs over, the one named last changes fastest.
Arguments:
- tangent: float32 [128, 128, 1024], P(('groups', 'lat')), parts along dimension 0, may hold values from -6 to 6
- wind_code: int32 [4, 128, 128], P(None, ('groups', 'lat')), parts along dimension 1, may hold values from 0 to 14
- courant: float32 [1024], replicated, may hold values from 0.2 to 0.8
- obs_index: int32 [32, 480], P(('groups', 'lat')), parts along dimension 0, may hold values from 0 to 511, as said below
- obs_count: int32 [32], P(('groups', 'lat')), parts along dimension 0, may hold values from 96 to 480, as said below
- obs_quality: bfloat16 [32, 480], P(('groups', 'lat')), parts along dimension 0, may hold values from 0.29882812 to 3
- background: bfloat16 [32, 480, 1024], P(('groups', 'lat')), parts along dimension 0, may hold values from -6 to 6
- w_first: bfloat16 [1024, 1024], replicated, may hold values from -0.1875 to 0.1875
- w_second: bfloat16 [1024, 1024], replicated, may hold values from -0.1875 to 0.1875
- w_third: bfloat16 [1024, 1024], replicated, may hold values from -0.1875 to 0.1875
- chan_weight: float32 [1024], replicated, may hold values from 0.3 to 3
Outputs:
- adjoint_field: float32 [128, 128, 1024], P(('groups', 'lat')), parts along dimension 0
There are 2 independent parts, one for each index of `groups`. A program takes and returns all parts, laid end to end along the dimension named above; an argument that names none is the same for every part. Nothing has to cross between parts.
Inputs may be any that keep to these rules, and one draw needn't show every extreme that they name: `obs_count`: the counts of all tiles sum to 192 times the number of tiles, and some tile has 480. `obs_index`: the 480 entries of one tile are distinct; the first obs_count of them are the observed columns.
All inputs are finite; a program needn't handle non-finite values.
Results may differ from a plain program's by a relative error of at most 0.0055.
Values may be sent and summed in bfloat16 or wider, within the bound.
No kernel may reach another device: no remote copies, remote signals or barrier semaphores. Data moves between devices by JAX's collectives and lax.ppermute only.
A program may use at most 64 MiB of HBM per device.

v0:
```python
import functools

import jax
import jax.numpy as jnp
from jax import lax
from jax.experimental import pallas as pl
from jax.experimental.pallas import tpu as pltpu
from jax.sharding import PartitionSpec as P

F32 = jnp.float32
BF16 = jnp.bfloat16
PART = 512
FAR_CELLS = 304
FAR_COLUMNS = 272
ANY = pl.BlockSpec(memory_space=pl.ANY)
VMEM = pl.BlockSpec(memory_space=pltpu.VMEM)
HBM = pl.BlockSpec(memory_space=pltpu.HBM)
SMEM = pl.BlockSpec(memory_space=pltpu.SMEM)
VMEM_LIMIT = 32 * 1024 * 1024
PACK_LIMIT = 60 * 1024 * 1024

OWN_BLOCKS = ((1, 1), (2, 1), (3, 0), (3, 1))
FAR_BLOCKS = ((0, 0), (0, 1), (1, 0), (2, 0))


def dot_t(left, right):
    return lax.dot_general(left, right, (((1,), (1,)), ((), ())), preferred_element_type=F32)


def dot(left, right):
    return jnp.dot(left, right, preferred_element_type=F32)


def store_sources(table, slot, codes, mirrored, sign, lon, rows):
    code = codes.astype(F32) - 1.0
    lat_q = jnp.where(code >= 5.0, 1.0, 0.0) + jnp.where(code >= 10.0, 1.0, 0.0)
    lon_step = code - 5.0 * lat_q - 2.0
    col = lax.broadcasted_iota(jnp.int32, code.shape, 1).astype(F32) - lon_step
    col = jnp.where(col < 0.0, col + lon, jnp.where(col >= lon, col - lon, col))
    stored = lax.broadcasted_iota(jnp.int32, code.shape, 0) & (rows - 1)
    row = (rows - 1 - stored) if mirrored else stored
    row = (row + slot * rows).astype(F32)
    src = (row - sign * (lat_q - 1.0)) * lon + col
    table[slot * code.shape[0] : (slot + 1) * code.shape[0], :] = jnp.where(code < 0.0, -65536.0, src)


def table_row(step, ext, rows):
    slot, at = ext // rows, ext % rows
    return slot * rows * rows + step * rows + (at if slot == 1 else rows - 1 - at)


def pull_matrix(out, turned, step, ext, lon, rows):
    span = 4 * lon
    lanes = lax.broadcasted_iota(jnp.int32, (lon, span), 1).astype(F32) + float((ext - 1) * lon)
    for half in range(2):
        k = table_row(step, ext + half, rows)
        column = turned[:, k : k + 1]
        out[half * lon : (half + 1) * lon, :] = jnp.where(column == lanes, 1.0, 0.0).astype(BF16)


def push_matrix(out, table, step, ext, lon, rows):
    dest = lax.broadcasted_iota(jnp.int32, (2 * lon, lon), 0).astype(F32) + float(ext * lon)
    for part in range(4):
        k = table_row(step, ext - 1 + part, rows)
        line = table[k : k + 1, :]
        out[:, part * lon : (part + 1) * lon] = jnp.where(line == dest, 1.0, 0.0).astype(BF16)


def wind_fields(codes, sign, rows):
    code = codes.astype(F32) - 1.0
    lat_q = jnp.where(code >= 5.0, 1.0, 0.0) + jnp.where(code >= 10.0, 1.0, 0.0)
    lat = jnp.where(code < 0.0, 9.0, sign * (lat_q - 1.0))
    lon = code - 5.0 * lat_q - 2.0
    fill = jnp.full((8 - rows, code.shape[1]), 9.0, F32)
    fields = []
    for step in range(code.shape[0] // rows):
        at = slice(step * rows, (step + 1) * rows)
        fields.append((jnp.concatenate([lat[at], fill], axis=0), jnp.concatenate([lon[at], fill], axis=0)))
    return fields


def shift_rows(mask, by):
    blank = jnp.zeros((1, mask.shape[1]), F32)
    if by == 1:
        return jnp.concatenate([blank, mask[:-1]], axis=0)
    if by == -1:
        return jnp.concatenate([mask[1:], blank], axis=0)
    return mask


def cells_pulled(fields, rows):
    lon = fields[0][0].shape[1]
    row = lax.broadcasted_iota(jnp.int32, (8, lon), 0)
    mask = jnp.where(row == 0, 1.0, 0.0)
    for lat, east in reversed(fields[: len(fields) - 1]):
        new = mask
        for a in (-1, 0, 1):
            total = jnp.zeros_like(mask)
            for b in range(-2, 3):
                hit = jnp.where((lat == float(a)) & (east == float(b)), mask, 0.0)
                total = jnp.maximum(total, hit if b == 0 else pltpu.roll(hit, (-b) % lon, 1))
            new = jnp.maximum(new, shift_rows(total, -a))
        mask = jnp.where(row < rows, new, 0.0)
    return mask


def cells_reached(fields, rows):
    lon = fields[0][0].shape[1]
    row = lax.broadcasted_iota(jnp.int32, (8, lon), 0)
    mask = jnp.zeros((8, lon), F32)
    for lat, east in fields:
        new = mask
        for a in (-1, 0, 1):
            source = shift_rows(mask, a)
            if a == 1:
                source = jnp.where(row == 0, 1.0, source)
            for b in range(-2, 3):
                seen = source if b == 0 else pltpu.roll(source, b % lon, 1)
                new = jnp.maximum(new, jnp.where((lat == float(a)) & (east == float(b)), seen, 0.0))
        mask = jnp.where(row < rows, new, 0.0)
    return mask


def slot_of(mask):
    lon = mask.shape[1]
    before = lax.broadcasted_iota(jnp.int32, (lon, lon), 0) < lax.broadcasted_iota(jnp.int32, (lon, lon), 1)
    place = dot(mask.astype(BF16), jnp.where(before, 1.0, 0.0).astype(BF16))
    totals = jnp.sum(mask, axis=1, keepdims=True)
    ahead = jnp.zeros((1, 1), F32)
    lines = []
    for j in range(mask.shape[0]):
        lines.append(place[j : j + 1] + ahead)
        ahead = ahead + totals[j : j + 1]
    return jnp.where(mask > 0.0, jnp.concatenate(lines, axis=0), -1.0), ahead


def choose_matrix(slots, size, rows, first=0):
    lon = slots.shape[1]
    at = lax.broadcasted_iota(jnp.int32, (size, lon), 0).astype(F32) + float(first)
    parts = [jnp.where(slots[j : j + 1] == at, 1.0, 0.0) for j in range(rows)]
    return jnp.concatenate(parts, axis=1).astype(BF16)


def spread_matrix(turned, row, size, first=0):
    at = lax.broadcasted_iota(jnp.int32, (turned.shape[0], size), 1).astype(F32) + float(first)
    return jnp.where(turned[:, row : row + 1] == at, 1.0, 0.0).astype(BF16)


def turn(slots):
    lon = slots.shape[1]
    return jnp.concatenate([slots, jnp.full((lon - slots.shape[0], lon), -1.0, F32)], axis=0).T


def sign_of(flip):
    return jnp.where(flip[0] == 1, -1.0, 1.0)


def pack_kernel(flip, tangent, wind, own, sent, codes, slots, buf, wind_b, sem):
    rows, lon = tangent.shape[0], tangent.shape[1]
    cells = rows * lon
    wind_copy = pltpu.make_async_copy(wind, wind_b, sem.at[rows])
    wind_copy.start()
    copies = []
    for j in range(rows):
        at = jnp.where(flip[0] == 1, rows - 1 - j, j)
        copies.append(pltpu.make_async_copy(tangent.at[at], buf.at[j], sem.at[j]))
        copies[-1].start()
    wind_copy.wait()
    for step in range(wind_b.shape[0]):
        for j in range(rows):
            code = jnp.where(flip[0] == 1, wind_b[step, rows - 1 - j : rows - j, :], wind_b[step, j : j + 1, :])
            codes[step * rows + j : step * rows + j + 1, :] = code.astype(F32) + 1.0
    mask = cells_pulled(wind_fields(codes[...], sign_of(flip), rows), rows)
    where, total = slot_of(mask)
    slots[...] = where
    head = codes.shape[0]
    capacity = sent.shape[0] - head
    tall = jnp.concatenate([mask, jnp.zeros((head - mask.shape[0], lon), F32)], axis=0)
    flag = jnp.broadcast_to(jnp.where(total > float(capacity), 1.0, 0.0), (head, lon))
    notes = jnp.concatenate([codes[...], tall, flag, jnp.zeros((head, own.shape[1] - 3 * lon), F32)], axis=1)
    notes = notes.astype(BF16)
    own[cells:, :] = notes
    sent[capacity:, :] = notes
    choose = choose_matrix(where, capacity, rows)
    for j in range(rows):
        copies[j].wait()
        own[j * lon : (j + 1) * lon, :] = buf[j].astype(BF16)
    sent[0:capacity, :] = dot(choose, own[0:cells, :]).astype(BF16)


def reach_kernel(flip, linked, own_slots, far_codes, far_slots, over):
    where, total = slot_of(cells_reached(wind_fields(far_codes[...], -sign_of(flip), 4), 4))
    far_slots[...] = where
    most = jnp.maximum(total, jnp.max(own_slots[...], axis=(0, 1), keepdims=True) + 1.0)
    over[0] = jnp.where(jnp.max(most) > float(FAR_COLUMNS), linked[0], 0)


def choose_kernel(flag, _one, _two, redone_one, redone_two, one, two, sem):
    @pl.when(flag[0] > 0)
    def _():
        copies = [
            pltpu.make_async_copy(redone_one, one, sem.at[0]),
            pltpu.make_async_copy(redone_two, two, sem.at[1]),
        ]
        for copy in copies:
            copy.start()
        for copy in copies:
            copy.wait()


def rest_kernel(first, slots, dense, out):
    rows = dense.shape[0] // slots.shape[1]
    cells = rows * slots.shape[1]
    choose = choose_matrix(slots[...], out.shape[0], rows, first)
    out[...] = dot(choose, dense[0:cells, :]).astype(BF16)


def blank_kernel(*outs):
    pass


def near_steps(mats, start_b, start_f, c_ref, outs, mid_b, mid_f, lon, cs):
    c = c_ref[0:1, cs]
    blocks = ((5, 7, 9), (6, 8), (7,))
    read_b, read_f, first = start_b, start_f, 4
    k = 0
    for step, exts in enumerate(blocks):
        for ext in exts:
            at = (ext - 1 - first) * lon
            pulled = dot(mats[k], read_b(at, 4 * lon))
            value = (1.0 - c) * read_f(at + lon, 2 * lon) + c * pulled
            k += 1
            if ext == exts[0]:
                outs[step][:, cs] = value
            if step < 2:
                to = (ext - exts[0]) * lon
                mid_f[step, to : to + 2 * lon, :] = value
                mid_b[step, to : to + 2 * lon, :] = value.astype(BF16)
        first = exts[0]
        read_b = functools.partial(lambda s, a, n: mid_b[s, a : a + n, :], step)
        read_f = functools.partial(lambda s, a, n: mid_f[s, a : a + n, :], step)


def by_parts(levels, body):
    @pl.loop(0, levels // PART)
    def _(i):
        body(pl.ds(pl.multiple_of(i * PART, PART), PART))


def far_steps(mats, start_b, start_f, c_ref, kept, mid_b, mid_f, lon, finish):
    c = c_ref[0:1, :]
    k = 0
    for step in range(4):
        now, last = step % 2, (step + 1) % 2
        for half in range(2):
            at = 2 * half * lon
            if step == 0:
                window, own = start_b(at, 4 * lon), start_f(at + lon, 2 * lon)
            else:
                window = mid_b[last, at : at + 4 * lon, :]
                own = mid_f[last, at + lon : at + 3 * lon, :]
            value = (1.0 - c) * own + c * dot(mats[k][...], window)
            k += 1
            if step < 3:
                mid_f[now, at : at + 2 * lon, :] = value
                mid_b[now, at : at + 2 * lon, :] = value.astype(BF16)
            else:
                finish(half, value)
        if step < 3:
            carried = kept[step][...]
            mid_f[now, 4 * lon :, :] = carried
            mid_b[now, 4 * lon :, :] = carried.astype(BF16)


def near_kernel(
    flip, obs_count, tangent, codes, near, courant, background, w_first, w_second, obs_index, obs_quality,
    slope_one, slope_two, kept_a, kept_b, kept_c, pick, place, place_far, near_codes, quality, slots, own_mats, own_f, own_b,
    table, mats, cells_b, mid_b, mid_f, hidden,
):
    rows, lon = tangent.shape[0], tangent.shape[1]
    cells = rows * lon
    sign = sign_of(flip)
    table[...] = jnp.zeros_like(table)
    near_codes[...] = near[cells:, 0:lon].astype(F32)
    store_sources(table, 1, codes[...], False, sign, lon, rows)
    store_sources(table, 2, near_codes[...], True, sign, lon, rows)
    turned = table[...].T
    k = 0
    for step, exts in enumerate(((5, 7, 9), (6, 8), (7,))):
        for ext in exts:
            pull_matrix(mats.at[k], turned, step, ext, lon, rows)
            k += 1
    for k, (step, half) in enumerate(OWN_BLOCKS):
        pull_matrix(own_mats.at[k], turned, step, step + 1 + 2 * half, lon, rows)
    for j in range(rows):
        row = tangent[jnp.where(flip[0] == 1, rows - 1 - j, j)]
        cells_b[j * lon : (j + 1) * lon, :] = row.astype(BF16)
        cells_b[(rows + j) * lon : (rows + j + 1) * lon, :] = near[(rows - 1 - j) * lon : (rows - j) * lon, :]

    own_f[...] = tangent[jnp.where(flip[0] == 1, rows - 1, 0)]
    own_b[...] = cells_b[0 : 2 * lon, :]

    def advect(cs):
        def start_f(at, size):
            pieces = []
            for row in range(at // lon, (at + size) // lon):
                if row < rows:
                    pieces.append(tangent[jnp.where(flip[0] == 1, rows - 1 - row, row), :, cs])
                else:
                    pieces.append(cells_b[row * lon : (row + 1) * lon, cs].astype(F32))
            return jnp.concatenate(pieces, axis=0)

        near_steps(
            mats, lambda at, size: cells_b[at : at + size, cs], start_f, courant,
            (kept_a, kept_b, kept_c), mid_b, mid_f, lon, cs,
        )

    by_parts(tangent.shape[2], advect)

    def first_layer(cs):
        first_tanh = jnp.tanh(dot(background[...], w_first[:, cs]))
        hidden[:, cs] = first_tanh.astype(BF16)
        slope_one[:, cs] = 1.0 - first_tanh * first_tanh

    by_parts(w_first.shape[1], first_layer)

    def second_layer(cs):
        second_tanh = jnp.tanh(dot(hidden[...], w_second[:, cs]))
        slope_two[:, cs] = 1.0 - second_tanh * second_tanh

    by_parts(w_second.shape[1], second_layer)

    count = obs_index.shape[1]
    at = obs_index[...]
    at = jnp.where(flip[0] == 1, at + (rows - 1 - 2 * lax.div(at, lon)) * lon, at)
    live = lax.broadcasted_iota(jnp.int32, at.shape, 1) < obs_count[0]
    at = jnp.where(live, at, -1)
    chosen = at == lax.broadcasted_iota(jnp.int32, (cells, count), 0)
    place[...] = jnp.where(chosen, 1.0, 0.0).astype(BF16)
    lines = jnp.concatenate([at.astype(F32), jnp.where(live, obs_quality[...].astype(F32), 0.0)], axis=0)
    lines = jnp.concatenate([lines, jnp.zeros((6, count), F32)], axis=0)
    lines = jnp.concatenate([lines, jnp.zeros((8, cells - count), F32)], axis=1).T
    quality[...] = lines[0:count, 1:2]
    columns = lax.broadcasted_iota(jnp.int32, (count, cells), 1).astype(F32)
    pick[...] = jnp.where(lines[0:count, 0:1] == columns, 1.0, 0.0).astype(BF16)
    where, _ = slot_of(cells_reached(wind_fields(codes[...], sign, rows), rows))
    slots[...] = where
    place_far[...] = dot(choose_matrix(slots[...], place_far.shape[0], rows), place[...]).astype(BF16)


def observe_kernel(
    redo, flip, linked, slots, own_f, own_b, codes, far, rest, courant, slope_one, slope_two, kept_a, kept_b, kept_c,
    hbm_first, hbm_second, hbm_third, pick, place, place_far, quality, chan_weight, own_mats,
    hbm_out, hbm_sent, hbm_codes, over,
    table, mats, cells_b, mid_b, mid_f, last_b, one_b, two_b, w_first, w_second, w_third, out, sent, far_codes, sem,
    rest_b,
):
    rows, lon = 4, own_f.shape[0]
    cells = rows * lon
    sign = sign_of(flip)
    capacity = far.shape[0] - codes.shape[0]
    loads = [
        pltpu.make_async_copy(hbm_first, w_first, sem.at[0]),
        pltpu.make_async_copy(hbm_second, w_second, sem.at[1]),
        pltpu.make_async_copy(hbm_third, w_third, sem.at[2]),
    ]
    for copy in loads:
        copy.start()
    table[...] = jnp.zeros_like(table)
    far_codes[...] = far[capacity:, 0:lon].astype(F32)
    store_sources(table, 0, far_codes[...], True, sign, lon, rows)
    store_sources(table, 1, codes[...], False, sign, lon, rows)
    turned = table[...].T
    keep_codes = pltpu.make_async_copy(far_codes, hbm_codes, sem.at[3])
    keep_codes.start()
    chosen = [None] * 8
    for k, (step, half) in enumerate(OWN_BLOCKS):
        chosen[2 * step + half] = own_mats.at[k]
    for k, (step, half) in enumerate(FAR_BLOCKS):
        pull_matrix(mats.at[k], turned, step, step + 1 + 2 * half, lon, rows)
        chosen[2 * step + half] = mats.at[k]
    where, _ = slot_of(far[capacity:, lon : 2 * lon].astype(F32)[0:8])
    where = turn(where)
    most = jnp.maximum(jnp.max(far[capacity:, 2 * lon : 3 * lon].astype(F32)), jnp.where(jnp.max(slots[...]) >= float(capacity), 1.0, 0.0))
    over[0] = jnp.where(most > 0.0, linked[0], 0)
    for j in range(rows):
        value = dot(spread_matrix(where, j, capacity), far[0:capacity, :])
        cells_b[(rows - 1 - j) * lon : (rows - j) * lon, :] = value.astype(BF16)
    cells_b[cells:, :] = own_b[...]

    if redo:
        copy = pltpu.make_async_copy(rest, rest_b, sem.at[5])
        copy.start()
        copy.wait()
        for j in range(rows):
            value = dot(spread_matrix(where, j, rest_b.shape[0], capacity), rest_b[...])
            at = slice((rows - 1 - j) * lon, (rows - j) * lon)
            cells_b[at, :] = (cells_b[at, :].astype(F32) + value).astype(BF16)

    def start_f(at, size):
        pieces = []
        for row in range(at // lon, (at + size) // lon):
            if row == rows:
                pieces.append(own_f[...])
            else:
                pieces.append(cells_b[row * lon : (row + 1) * lon, :].astype(F32))
        return jnp.concatenate(pieces, axis=0)

    def finish(half, value):
        last_b[2 * half * lon : 2 * (half + 1) * lon, :] = value.astype(BF16)

    far_steps(
        chosen, lambda at, size: cells_b[at : at + size, :], start_f, courant,
        (kept_a, kept_b, kept_c), mid_b, mid_f, lon, finish,
    )
    one_b[...] = dot(pick[...], last_b[...]).astype(BF16)
    loads[0].wait()
    two_b[...] = (slope_one[...] * dot(one_b[...], w_first[...])).astype(BF16)
    loads[1].wait()
    one_b[...] = (slope_two[...] * dot(two_b[...], w_second[...])).astype(BF16)
    loads[2].wait()
    scale = quality[...] * chan_weight[0:1, :]
    two_b[...] = (scale * dot(one_b[...], w_third[...])).astype(BF16)
    one_b[...] = (slope_two[...] * dot_t(two_b[...], w_third[...])).astype(BF16)
    two_b[...] = (slope_one[...] * dot_t(one_b[...], w_second[...])).astype(BF16)
    one_b[...] = dot_t(two_b[...], w_first[...]).astype(BF16)
    sent[...] = dot(place_far[...], one_b[...]).astype(BF16)
    keep_sent = pltpu.make_async_copy(sent, hbm_sent, sem.at[4])
    keep_sent.start()
    out[...] = dot(place[...], one_b[...]).astype(BF16)
    keep_out = pltpu.make_async_copy(out, hbm_out, sem.at[0])
    keep_out.start()
    keep_codes.wait()
    keep_sent.wait()
    keep_out.wait()


def near_adjoint_kernel(
    flip, rest, cells_own, cells_near, codes, near_codes, far_codes, far_slots, courant,
    kept_a, kept_b, kept_c, far_mats, spread,
    table, mats, cells_b, mid_b, mid_f,
):
    rows, lon = 4, table.shape[1]
    cells = rows * lon
    sign = sign_of(flip)
    store_sources(table, 0, far_codes[...], True, sign, lon, rows)
    store_sources(table, 1, codes[...], False, sign, lon, rows)
    store_sources(table, 2, near_codes[...], True, sign, lon, rows)
    k = 0
    for order, exts in enumerate(((5, 7, 9), (6, 8), (7,))):
        for ext in exts:
            push_matrix(mats.at[k], table, 3 - order, ext, lon, rows)
            k += 1
    cells_b[0:cells, :] = cells_own[...]
    for j in range(rows):
        cells_b[(rows + j) * lon : (rows + j + 1) * lon, :] = cells_near[
            (rows - 1 - j) * lon : (rows - j) * lon, :
        ]

    def advect(cs):
        near_steps(
            mats, lambda at, size: cells_b[at : at + size, cs],
            lambda at, size: cells_b[at : at + size, cs].astype(F32), courant,
            (kept_a, kept_b, kept_c), mid_b, mid_f, lon, cs,
        )

    by_parts(cells_own.shape[1], advect)
    for order in range(4):
        for half in range(2):
            push_matrix(far_mats.at[2 * order + half], table, 3 - order, order + 1 + 2 * half, lon, rows)
    where = turn(far_slots[...])
    capacity = spread.shape[1]
    for j in range(rows):
        spread[j * lon : (j + 1) * lon, :] = spread_matrix(where, j, capacity)


def far_adjoint_kernel(
    flip, flag, cells_own, far, rest, courant, kept_a, kept_b, kept_c, mats, spread, far_slots,
    out,
    cells_b, mid_b, mid_f, result, rest_b, sem,
):
    rows, lon = out.shape[0], out.shape[1]
    cells = rows * lon
    for j in range(rows):
        value = dot(spread[j * lon : (j + 1) * lon, :], far[...])
        cells_b[(rows - 1 - j) * lon : (rows - j) * lon, :] = value.astype(BF16)
    cells_b[cells:, :] = cells_own[0 : 2 * lon, :]

    @pl.when(flag[0] > 0)
    def _():
        copy = pltpu.make_async_copy(rest, rest_b, sem.at[rows])
        copy.start()
        copy.wait()
        where = turn(far_slots[...])
        for j in range(rows):
            value = dot(spread_matrix(where, j, rest_b.shape[0], spread.shape[1]), rest_b[...])
            at = slice((rows - 1 - j) * lon, (rows - j) * lon)
            cells_b[at, :] = (cells_b[at, :].astype(F32) + value).astype(BF16)

    copies = []

    def finish(half, value):
        for part in range(2):
            j = 2 * half + part
            result[j] = value[part * lon : (part + 1) * lon, :]
            at = jnp.where(flip[0] == 1, rows - 1 - j, j)
            copies.append(pltpu.make_async_copy(result.at[j], out.at[at], sem.at[j]))
            copies[-1].start()

    far_steps(
        [mats.at[k] for k in range(8)], lambda at, size: cells_b[at : at + size, :],
        lambda at, size: cells_b[at : at + size, :].astype(F32), courant,
        (kept_a, kept_b, kept_c), mid_b, mid_f, lon, finish,
    )
    for copy in copies:
        copy.wait()


def params():
    return pltpu.CompilerParams(vmem_limit_bytes=VMEM_LIMIT)


def shape(dims, dtype):
    return jax.ShapeDtypeStruct(dims, dtype)


def send_rest(first, slots, dense, size, links):
    rest = pl.pallas_call(
        functools.partial(rest_kernel, first),
        out_shape=shape((size, dense.shape[1]), BF16),
        in_specs=[VMEM, VMEM],
        out_specs=VMEM,
        name="rest",
    )(slots, dense)
    return lax.ppermute(rest, "lat", links)


def blank(outs):
    return pl.pallas_call(blank_kernel, out_shape=outs, out_specs=[ANY] * len(outs), name="blank")()


def local(
    tangent,
    wind_code,
    courant,
    obs_index,
    obs_count,
    obs_quality,
    background,
    w_first,
    w_second,
    w_third,
    chan_weight,
):
    rows, lon, levels = tangent.shape
    cells = rows * lon
    head = wind_code.shape[0] * rows
    listed = obs_index.shape[1]
    hidden_size = w_first.shape[1]
    count = lax.axis_size("lat")
    here = lax.axis_index("lat")
    odd = (here % 2).astype(jnp.int32)
    flip = odd.reshape(1)
    linked = ((here > 0) & (here < count - 1)).astype(jnp.int32).reshape(1)
    pairs = [(i, i ^ 1) for i in range(count)]
    links = [(i, i + 1) for i in range(1, count - 1, 2)]
    links = links + [(b, a) for a, b in links]

    own, sent, codes, slots = pl.pallas_call(
        pack_kernel,
        out_shape=[
            shape((cells + head, levels), BF16),
            shape((FAR_CELLS + head, levels), BF16),
            shape((head, lon), F32),
            shape((8, lon), F32),
        ],
        in_specs=[SMEM, HBM, HBM],
        out_specs=[VMEM] * 4,
        scratch_shapes=[
            pltpu.VMEM((rows, lon, levels), F32),
            pltpu.VMEM(wind_code.shape, jnp.int32),
            pltpu.SemaphoreType.DMA((rows + 1,)),
        ],
        compiler_params=pltpu.CompilerParams(vmem_limit_bytes=PACK_LIMIT),
        name="pack",
    )(flip, tangent, wind_code)

    far = lax.ppermute(sent, "lat", links)
    near = lax.ppermute(own, "lat", pairs)

    c_row = courant.reshape(1, levels)
    kept_shape = [shape((2 * lon, levels), F32)] * 3
    slope_shape = shape((listed, hidden_size), F32)

    def run_near():
        return pl.pallas_call(
            near_kernel,
            out_shape=[slope_shape, slope_shape]
            + kept_shape
            + [
                shape((listed, cells), BF16),
                shape((cells, listed), BF16),
                shape((FAR_COLUMNS, listed), BF16),
                shape((head, lon), F32),
                shape((listed, 1), F32),
                shape((8, lon), F32),
                shape((4, 2 * lon, 4 * lon), BF16),
                shape((lon, levels), F32),
                shape((2 * lon, levels), BF16),
            ],
            in_specs=[SMEM, SMEM] + [VMEM] * 9,
            out_specs=[VMEM] * 14,
            scratch_shapes=[
                pltpu.VMEM((lon, lon), F32),
                pltpu.VMEM((6, 2 * lon, 4 * lon), BF16),
                pltpu.VMEM((2 * cells, levels), BF16),
                pltpu.VMEM((2, 6 * lon, PART), BF16),
                pltpu.VMEM((2, 6 * lon, PART), F32),
                pltpu.VMEM((listed, hidden_size), BF16),
            ],
            compiler_params=params(),
            cost_estimate=pl.CostEstimate(flops=4_000_000_000, bytes_accessed=16_000_000, transcendentals=1_000_000),
            name="near",
        )(
            flip, obs_count, tangent, codes, near, c_row, background[0], w_first, w_second, obs_index, obs_quality,
        )

    column_shape = [pltpu.HBM((cells, levels), BF16), pltpu.HBM((FAR_COLUMNS, levels), BF16)]

    def run_observe(redo, parts, rest):
        slope_one, slope_two, kept_a, kept_b, kept_c, pick, place, place_far = parts[:8]
        quality, _, own_mats, own_f, own_b = parts[9:]
        rest_specs = [ANY] if redo else []
        body = functools.partial(observe_kernel, redo)
        rest_args = [rest] if redo else []
        rest_scratch = [pltpu.VMEM((cells - FAR_CELLS, levels), BF16)]

        def kernel(*refs):
            refs = list(refs)
            if not redo:
                refs.insert(7, None)
                refs.append(None)
            body(*refs)

        return pl.pallas_call(
            kernel,
            out_shape=column_shape + [pltpu.HBM((head, lon), F32), shape((1,), jnp.int32)],
            in_specs=[SMEM, SMEM] + [VMEM] * 5 + rest_specs + [VMEM] * 6 + [ANY] * 3 + [VMEM] * 6,
            out_specs=[HBM] * 3 + [SMEM],
            scratch_shapes=[
                pltpu.VMEM((lon, lon), F32),
                pltpu.VMEM((4, 2 * lon, 4 * lon), BF16),
                pltpu.VMEM((6 * lon, levels), BF16),
                pltpu.VMEM((2, 6 * lon, levels), BF16),
                pltpu.VMEM((2, 6 * lon, levels), F32),
                pltpu.VMEM((cells, levels), BF16),
                pltpu.VMEM((listed, levels), BF16),
                pltpu.VMEM((listed, levels), BF16),
                pltpu.VMEM(w_first.shape, BF16),
                pltpu.VMEM(w_second.shape, BF16),
                pltpu.VMEM(w_third.shape, BF16),
                pltpu.VMEM((cells, levels), BF16),
                pltpu.VMEM((FAR_COLUMNS, levels), BF16),
                pltpu.VMEM((head, lon), F32),
                pltpu.SemaphoreType.DMA((6,)),
            ]
            + (rest_scratch if redo else []),
            compiler_params=params(),
            name="observe",
        )(
            flip, linked, slots, own_f, own_b, codes, far, *rest_args, c_row,
            slope_one, slope_two, kept_a, kept_b, kept_c, w_first, w_second, w_third,
            pick, place, place_far, quality, chan_weight.reshape(1, -1), own_mats,
        )

    parts = run_near()
    near_codes, own_slots = parts[8], parts[10]
    cells_own, sent, far_codes, over = run_observe(False, parts, None)

    def observe_again():
        rest = send_rest(FAR_CELLS, slots, own, cells - FAR_CELLS, links)
        return run_observe(True, run_near(), rest)[:2]

    redone = lax.cond(over[0] > 0, observe_again, lambda: blank(column_shape))
    cells_own, sent = pl.pallas_call(
        choose_kernel,
        out_shape=column_shape,
        in_specs=[SMEM] + [HBM] * 4,
        out_specs=[HBM] * 2,
        scratch_shapes=[pltpu.SemaphoreType.DMA((2,))],
        input_output_aliases={1: 0, 2: 1},
        name="choose",
    )(over, cells_own, sent, *redone)

    columns_far = lax.ppermute(sent, "lat", links)
    cells_near = lax.ppermute(cells_own, "lat", pairs)

    far_slots, over = pl.pallas_call(
        reach_kernel,
        out_shape=[shape((8, lon), F32), shape((1,), jnp.int32)],
        in_specs=[SMEM, SMEM, VMEM, VMEM],
        out_specs=[VMEM, SMEM],
        name="reach",
    )(flip, linked, own_slots, far_codes)
    left = cells - FAR_COLUMNS
    rest = lax.cond(
        over[0] > 0,
        lambda: send_rest(FAR_COLUMNS, own_slots, cells_own, left, links),
        lambda: blank([shape((left, levels), BF16)])[0],
    )
    kept_a, kept_b, kept_c, mats, spread = pl.pallas_call(
        near_adjoint_kernel,
        out_shape=kept_shape
        + [
            shape((8, 2 * lon, 4 * lon), BF16),
            shape((cells, FAR_COLUMNS), BF16),
        ],
        in_specs=[SMEM, ANY] + [VMEM] * 7,
        out_specs=[VMEM] * 5,
        scratch_shapes=[
            pltpu.VMEM((lon, lon), F32),
            pltpu.VMEM((6, 2 * lon, 4 * lon), BF16),
            pltpu.VMEM((2 * cells, levels), BF16),
            pltpu.VMEM((2, 6 * lon, PART), BF16),
            pltpu.VMEM((2, 6 * lon, PART), F32),
        ],
        compiler_params=params(),
        cost_estimate=pl.CostEstimate(flops=2_000_000_000, bytes_accessed=8_000_000, transcendentals=0),
        name="near_adjoint",
    )(flip, rest, cells_own, cells_near, codes, near_codes, far_codes, far_slots, c_row)

    return pl.pallas_call(
        far_adjoint_kernel,
        out_shape=shape((rows, lon, levels), F32),
        in_specs=[SMEM, SMEM, VMEM, VMEM, ANY] + [VMEM] * 7,
        out_specs=HBM,
        scratch_shapes=[
            pltpu.VMEM((6 * lon, levels), BF16),
            pltpu.VMEM((2, 6 * lon, levels), BF16),
            pltpu.VMEM((2, 6 * lon, levels), F32),
            pltpu.VMEM((rows, lon, levels), F32),
            pltpu.VMEM((cells - FAR_COLUMNS, levels), BF16),
            pltpu.SemaphoreType.DMA((rows + 1,)),
        ],
        compiler_params=params(),
        name="far_adjoint",
    )(
        flip, over, cells_own, columns_far, rest, c_row,
        kept_a, kept_b, kept_c, mats, spread, far_slots,
    )


def solution(mesh):
    placed = (
        P(("groups", "lat"), None, None),
        P(None, ("groups", "lat"), None),
        P(),
        P(("groups", "lat"), None),
        P(("groups", "lat")),
        P(("groups", "lat"), None),
        P(("groups", "lat"), None, None),
        P(),
        P(),
        P(),
        P(),
    )
    return jax.shard_map(
        local,
        mesh=mesh,
        in_specs=placed,
        out_specs=P(("groups", "lat"), None, None),
        check_vma=False,
    )
```

profile of v0, /device:TPU:25, one launch (start us, length us, event | category | flops | bytes accessed | tf_op | source)
XLA Modules:
  0.0 59.9 jit_solution(10865446625374048729)
XLA Ops:
  0.0 0.0 copy-start.3
  0.0 0.0 copy-start.7
  0.0 0.0 copy-start.6
  0.0 0.0 copy-start.4
  0.0 3.1 %pack.1 = (bf16[528,1024]{1,0:T(8,128)(2,1)}, bf16[320,1024]{1,0:T(8,128)(2,1)}, f32[16,128]{1,0:T(8,128)S(1)}, f32[8,128]{1,0:T(8,128)S(1)}) custom-call(s32[1]{0:T(128)} %bitcast.2.flip.refs_0_, f32[4,128,1024]{2,1,0:T(8,128)} %tangent.3, s32[4,4,128]{2,1,0:T(4,128)} %wind.1), custom_call_target="tpu_custom_call" | custom-call | tf_op jit(solution)/shard_map/pack/pallas_call | solution.py:569
  3.2 0.7 %collective-permute-start.2 = (bf16[528,1024]{1,0:T(8,128)(2,1)}, bf16[528,1024]{1,0:T(8,128)(2,1)}, u32[]{:S(2)}, u32[]{:S(2)}) collective-permute-start(bf16[528,1024]{1,0:T(8,128)(2,1)} %get-tuple-element.113), channel_id=1, source_target_pairs={{0,1},{1,0},{2,3},{3,2},{4,5},{5,4},{6,7},{7,6},{8,9},{9,8},{10,11... | collective-permute-start | bytes 3244040 | tf_op jit(solution)/shard_map/ppermute | solution.py:589
  3.9 3.0 %collective-permute-start.3 = (bf16[320,1024]{1,0:T(8,128)(2,1)}, bf16[320,1024]{1,0:T(8,128)(2,1)S(1)}, u32[]{:S(2)}, u32[]{:S(2)}) collective-permute-start(bf16[320,1024]{1,0:T(8,128)(2,1)} %get-tuple-element.118), channel_id=1, source_target_pairs={{1,2},{3,4},{5,6},{7,8},{9,10},{11,12},{13,14},{2,1},{4,3},{6,5},{... | collective-permute-start | bytes 1966088 | tf_op jit(solution)/shard_map/ppermute | solution.py:588
  7.6 0.0 collective-permute-done.2.near
  7.6 0.0 copy-done.3
  7.6 0.0 copy-done.7
  7.7 0.0 copy-done.6
  7.7 0.0 copy-done.4
  7.7 0.0 copy-start.5
  7.7 9.5 %near.3 = (f32[480,1024]{1,0:T(8,128)S(1)}, f32[480,1024]{1,0:T(8,128)S(1)}, f32[256,1024]{1,0:T(8,128)S(1)}, f32[256,1024]{1,0:T(8,128)S(1)}, f32[256,1024]{1,0...) custom-call(s32[1]{0:T(128)} %bitcast.2.flip.refs_0_, ...), custom_call_target="tpu_custom_call" | custom-call | flops 4000000000 | bytes 16000000 | tf_op jit(solution)/shard_map/near/pallas_call | solution.py:596
  17.2 5.8 %collective-permute-done.3.refs_6_ = bf16[320,1024]{1,0:T(8,128)(2,1)S(1)} collective-permute-done((bf16[320,1024]{1,0:T(8,128)(2,1)}, bf16[320,1024]{1,0:T(8,128)(2,1)S(1)}, u32[]{:S(2)}, u32[]{:S(2)}) %collective-permute-start.3) | collective-permute-done | bytes 655392 | tf_op jit(solution)/shard_map/ppermute | solution.py:588
  23.0 0.0 copy-done.5
  23.0 13.1 %observe.3 = (bf16[512,1024]{1,0:T(8,128)(2,1)}, bf16[272,1024]{1,0:T(8,128)(2,1)}, f32[16,128]{1,0:T(8,128)}, s32[1]{0:T(128)}) custom-call(s32[1]{0:T(128)} %bitcast.2.flip.refs_0_, s32[1]{0:T(128)} %bitcast.3.refs_1_.linked, f32[8,128]{1,0:T(8,128)S(1)} %get-tuple-element.115.refs_2_, f32[128,1024]{1,0:T(8,128)S(1)} %get-tuple-element.116.refs_3_, ...), custom_call_target="tpu_custom_call" | custom-call | tf_op jit(solution)/shard_map/observe/pallas_call | solution.py:645
  36.7 0.2 conditional.2
  37.0 0.0 copy-start
  37.0 0.7 %choose.1 = (bf16[512,1024]{1,0:T(8,128)(2,1)}, bf16[272,1024]{1,0:T(8,128)(2,1)}) custom-call(s32[1]{0:T(128)} %get-tuple-element.131.flag, bf16[512,1024]{1,0:T(8,128)(2,1)} %get-tuple-element.132._one, bf16[272,1024]{1,0:T(8,128)(2,1)} %get-tuple-element.133._two, ...), custom_call_target="tpu_custom_call", output_to_operand_aliasing={{0}: (1, {}), {1}: (2, {})} | custom-call | tf_op jit(solution)/shard_map/choose/pallas_call | solution.py:685
  37.7 0.1 collective-permute-start.5
  37.7 1.9 %collective-permute-start.4 = (bf16[272,1024]{1,0:T(8,128)(2,1)}, bf16[272,1024]{1,0:T(8,128)(2,1)S(1)}, u32[]{:S(2)}, u32[]{:S(2)}) collective-permute-start(bf16[272,1024]{1,0:T(8,128)(2,1)} %get-tuple-element.137), channel_id=1, source_target_pairs={{1,2},{3,4},{5,6},{7,8},{9,10},{11,12},{13,14},{2,1},{4,3},{6,5},{... | collective-permute-start | bytes 1671176 | tf_op jit(solution)/shard_map/ppermute | solution.py:695
  39.7 1.8 %reach.1 = (f32[8,128]{1,0:T(8,128)}, s32[1]{0:T(128)}) custom-call(s32[1]{0:T(128)} %bitcast.2.flip.refs_0_, s32[1]{0:T(128)} %bitcast.3.refs_1_.linked, f32[8,128]{1,0:T(8,128)S(1)} %get-tuple-element.114.own_slots, f32[16,128]{1,0:T(8,128)} %get-tuple-element.129.far_codes), custom_call_target="tpu_custom_call" | custom-call | tf_op jit(solution)/shard_map/reach/pallas_call | solution.py:698
  42.2 0.0 collective-permute-done.5.cells_near
  42.2 0.0 copy-done
  42.2 0.0 copy-start.1
  42.2 0.7 %copy-done.1 = f32[8,128]{1,0:T(8,128)S(1)} copy-done((f32[8,128]{1,0:T(8,128)S(1)}, f32[8,128]{1,0:T(8,128)}, u32[]{:S(2)}) %copy-start.1) | copy-done | bytes 4120
  42.9 0.0 copy-start.2
  42.9 5.2 %near_adjoint.1 = (f32[256,1024]{1,0:T(8,128)S(1)}, f32[256,1024]{1,0:T(8,128)S(1)}, f32[256,1024]{1,0:T(8,128)S(1)}, bf16[8,256,512]{2,1,0:T(8,128)(2,1)S(1)}, bf16[512,272]{1,0:T(8,128)(2,1)S(1)}) custom-call(s32[1]{0:T(128)} %bitcast.2.flip.refs_0_, bf16[240,1024]{1,0:T(8,128)(2,1)} %get-tuple-element.150.rest, ...), custom_call_target="tpu_custom_call" | custom-call | flops 2000000000 | bytes 8000000 | tf_op jit(solution)/shard_map/near_adjoint/pallas_call | solution.py:711
  48.1 6.7 %collective-permute-done.4.far = bf16[272,1024]{1,0:T(8,128)(2,1)S(1)} collective-permute-done((bf16[272,1024]{1,0:T(8,128)(2,1)}, bf16[272,1024]{1,0:T(8,128)(2,1)S(1)}, u32[]{:S(2)}, u32[]{:S(2)}) %collective-permute-start.4) | collective-permute-done | bytes 557088 | tf_op jit(solution)/shard_map/ppermute | solution.py:695
  54.8 0.0 copy-done.2
  54.8 4.9 %far_adjoint.1 = f32[4,128,1024]{2,1,0:T(8,128)} custom-call(s32[1]{0:T(128)} %bitcast.2.flip.refs_0_, s32[1]{0:T(128)} %get-tuple-element.130.flag, bf16[512,1024]{1,0:T(8,128)(2,1)S(1)} %copy-done.2, bf16[272,1024]{1,0:T(8,128)(2,1)S(1)} %collective-permute-done.4.far, bf16[240,1024]{1,0:T(8,128)(2,1)} %get-tuple-element.150.rest, f32[1,1024]{1,0:T(1,128)S(1)} %bitcast.13, ...), custom_call_target="tpu_custom_call" | custom-call | tf_op jit(solution)/shard_map/far_adjoint/pallas_call | solution.py:732
  (3 shorter events, 0.0 us)
Async XLA Ops:
  0.0 7.6 %copy-start.3 = (f32[4,128,1024]{2,1,0:T(8,128)S(1)}, f32[4,128,1024]{2,1,0:T(8,128)}, u32[]{:S(2)}) copy-start(f32[4,128,1024]{2,1,0:T(8,128)} %tangent.3) | copy-start | bytes 6291460
  0.0 7.6 %copy-start.7 = (bf16[1,480]{1,0:T(2,128)(2,1)S(1)}, bf16[1,480]{1,0:T(2,128)(2,1)}, u32[]{:S(2)}) copy-start(bf16[1,480]{1,0:T(2,128)(2,1)} %obs_quality.1) | copy-start | bytes 2884
  0.0 7.6 %copy-start.6 = (s32[1,480]{1,0:T(1,128)S(1)}, s32[1,480]{1,0:T(1,128)}, u32[]{:S(2)}) copy-start(s32[1,480]{1,0:T(1,128)} %obs_index.1) | copy-start | bytes 5764
  0.0 7.7 %copy-start.4 = (f32[1024]{0:T(1024)S(1)}, f32[1024]{0:T(1024)}, u32[]{:S(2)}) copy-start(f32[1024]{0:T(1024)} %param.17) | copy-start | bytes 12292
  3.2 4.5 %collective-permute-start.2 = (bf16[528,1024]{1,0:T(8,128)(2,1)}, bf16[528,1024]{1,0:T(8,128)(2,1)}, u32[]{:S(2)}, u32[]{:S(2)}) collective-permute-start(bf16[528,1024]{1,0:T(8,128)(2,1)} %get-tuple-element.113), channel_id=1, source_target_pairs={{0,1},{1,0},{2,3},{3,2},{4,5},{5,4},{6,7},{7,6},{8,9},{9,8},{10,11... | collective-permute-start | bytes 3244040 | tf_op jit(solution)/shard_map/ppermute | solution.py:589
  3.9 19.1 %collective-permute-start.3 = (bf16[320,1024]{1,0:T(8,128)(2,1)}, bf16[320,1024]{1,0:T(8,128)(2,1)S(1)}, u32[]{:S(2)}, u32[]{:S(2)}) collective-permute-start(bf16[320,1024]{1,0:T(8,128)(2,1)} %get-tuple-element.118), channel_id=1, source_target_pairs={{1,2},{3,4},{5,6},{7,8},{9,10},{11,12},{13,14},{2,1},{4,3},{6,5},{... | collective-permute-start | bytes 1966088 | tf_op jit(solution)/shard_map/ppermute | solution.py:588
  7.7 15.4 %copy-start.5 = (f32[1024]{0:T(1024)S(1)}, f32[1024]{0:T(1024)}, u32[]{:S(2)}) copy-start(f32[1024]{0:T(1024)} %param.25) | copy-start | bytes 12292
  37.0 5.2 %copy-start = (f32[16,128]{1,0:T(8,128)S(1)}, f32[16,128]{1,0:T(8,128)}, u32[]{:S(2)}) copy-start(f32[16,128]{1,0:T(8,128)} %get-tuple-element.129.far_codes) | copy-start | bytes 24580
  37.7 4.5 %collective-permute-start.5 = (bf16[512,1024]{1,0:T(8,128)(2,1)}, bf16[512,1024]{1,0:T(8,128)(2,1)S(1)}, u32[]{:S(2)}, u32[]{:S(2)}) collective-permute-start(bf16[512,1024]{1,0:T(8,128)(2,1)} %get-tuple-element.136.cells_own), channel_id=1, source_target_pairs={{0,1},{1,0},{2,3},{3,2},{4,5},{5,4},{6,7},{7,6},{8,9},{9,8},{10,11... | collective-permute-start | bytes 3145736 | tf_op jit(solution)/shard_map/ppermute | solution.py:696
  37.7 17.0 %collective-permute-start.4 = (bf16[272,1024]{1,0:T(8,128)(2,1)}, bf16[272,1024]{1,0:T(8,128)(2,1)S(1)}, u32[]{:S(2)}, u32[]{:S(2)}) collective-permute-start(bf16[272,1024]{1,0:T(8,128)(2,1)} %get-tuple-element.137), channel_id=1, source_target_pairs={{1,2},{3,4},{5,6},{7,8},{9,10},{11,12},{13,14},{2,1},{4,3},{6,5},{... | collective-permute-start | bytes 1671176 | tf_op jit(solution)/shard_map/ppermute | solution.py:695
  42.2 0.7 %copy-start.1 = (f32[8,128]{1,0:T(8,128)S(1)}, f32[8,128]{1,0:T(8,128)}, u32[]{:S(2)}) copy-start(f32[8,128]{1,0:T(8,128)} %get-tuple-element.139.far_slots) | copy-start | bytes 12292
  42.9 11.9 %copy-start.2 = (bf16[512,1024]{1,0:T(8,128)(2,1)S(1)}, bf16[512,1024]{1,0:T(8,128)(2,1)}, u32[]{:S(2)}) copy-start(bf16[512,1024]{1,0:T(8,128)(2,1)} %get-tuple-element.136.cells_own) | copy-start | bytes 3145732
where the time goes:
time: 60.2 us; the launch traced here: 59.9 us
  Pallas kernels  38.3 us (64%)
  waiting for transfers between devices  12.5 us (21%)
  starting transfers between devices  5.78 us (10%)
  between operations  2.33 us (4%)
  local copies, waits for them, and re-layouts  0.7 us (1%)
    pallas_call x1, Pallas kernels, run_observe(): pl.pallas_call(kernel, out_shape=column_shape + [pltpu.HBM((head, lon), F...  13.1 us
    pallas_call x1, Pallas kernels, run_near(): pl.pallas_call(near_kernel, out_shape=[slope_shape, slope_shape] + kept_s...  9.54 us
    ppermute x1, waiting for transfers between devices, local(): columns_far = lax.ppermute(sent, 'lat', links)  6.71 us
    ppermute x1, waiting for transfers between devices, local(): far = lax.ppermute(sent, 'lat', links)  5.81 us
    pallas_call x1, Pallas kernels, local(): pl.pallas_call(near_adjoint_kernel, out_shape=kept_shape + [shape((8, 2 *...  5.17 us
    pallas_call x1, Pallas kernels, local(): pl.pallas_call(far_adjoint_kernel, out_shape=shape((rows, lon, levels), F...  4.92 us
    pallas_call x1, Pallas kernels, local(): pl.pallas_call(pack_kernel, out_shape=[shape((cells + head, levels), BF16...  3.13 us
    ppermute x1, starting transfers between devices, local(): far = lax.ppermute(sent, 'lat', links)  3.05 us
  transfers between devices with their start and end apart: 4, of which 2 were waited for; matrix products, arithmetic and copies ran while one was open for 0% of the time, Pallas kernels for 28%

commit v1 on v0

--- a/solution.py
+++ b/solution.py
@@ -11,7 +11,7 @@
 BF16 = jnp.bfloat16
 PART = 512
 FAR_CELLS = 304
-FAR_COLUMNS = 272
+FAR_COLUMNS = 256
 ANY = pl.BlockSpec(memory_space=pl.ANY)
 VMEM = pl.BlockSpec(memory_space=pltpu.VMEM)
 HBM = pl.BlockSpec(memory_space=pltpu.HBM)
@@ -188,20 +188,13 @@
     sent[0:capacity, :] = dot(choose, own[0:cells, :]).astype(BF16)
 
 
-def reach_kernel(flip, linked, own_slots, far_codes, far_slots, over):
-    where, total = slot_of(cells_reached(wind_fields(far_codes[...], -sign_of(flip), 4), 4))
-    far_slots[...] = where
-    most = jnp.maximum(total, jnp.max(own_slots[...], axis=(0, 1), keepdims=True) + 1.0)
-    over[0] = jnp.where(jnp.max(most) > float(FAR_COLUMNS), linked[0], 0)
-
-
-def choose_kernel(flag, _one, _two, redone_one, redone_two, one, two, sem):
+def choose_kernel(flag, *refs):
+    count = len(refs) // 3
+    redone, outs, sem = refs[count : 2 * count], refs[2 * count : 3 * count], refs[-1]
+
     @pl.when(flag[0] > 0)
     def _():
-        copies = [
-            pltpu.make_async_copy(redone_one, one, sem.at[0]),
-            pltpu.make_async_copy(redone_two, two, sem.at[1]),
-        ]
+        copies = [pltpu.make_async_copy(redone[k], outs[k], sem.at[k]) for k in range(count)]
         for copy in copies:
             copy.start()
         for copy in copies:
@@ -350,9 +343,9 @@
 
 def observe_kernel(
     redo, flip, linked, slots, own_f, own_b, codes, far, rest, courant, slope_one, slope_two, kept_a, kept_b, kept_c,
-    hbm_first, hbm_second, hbm_third, pick, place, place_far, quality, chan_weight, own_mats,
-    hbm_out, hbm_sent, hbm_codes, over,
-    table, mats, cells_b, mid_b, mid_f, last_b, one_b, two_b, w_first, w_second, w_third, out, sent, far_codes, sem,
+    hbm_first, hbm_second, hbm_third, pick, place, place_far, quality, chan_weight, own_mats, own_slots,
+    hbm_out, hbm_low, hbm_high, hbm_codes, hbm_slots, over, over_columns,
+    table, mats, cells_b, mid_b, mid_f, last_b, one_b, two_b, w_first, w_second, w_third, out, low, high, far_codes, far_slots, sem,
     rest_b,
 ):
     rows, lon = 4, own_f.shape[0]
@@ -373,6 +366,12 @@
     turned = table[...].T
     keep_codes = pltpu.make_async_copy(far_codes, hbm_codes, sem.at[3])
     keep_codes.start()
+    reached, total = slot_of(cells_reached(wind_fields(far_codes[...], -sign, rows), rows))
+    far_slots[...] = reached
+    keep_slots = pltpu.make_async_copy(far_slots, hbm_slots, sem.at[6])
+    keep_slots.start()
+    most = jnp.maximum(jnp.max(total), jnp.max(own_slots[...]) + 1.0)
+    over_columns[0] = jnp.where(most > float(FAR_COLUMNS), linked[0], 0)
     chosen = [None] * 8
     for k, (step, half) in enumerate(OWN_BLOCKS):
         chosen[2 * step + half] = own_mats.at[k]
@@ -424,26 +423,39 @@
     one_b[...] = (slope_two[...] * dot_t(two_b[...], w_third[...])).astype(BF16)
     two_b[...] = (slope_one[...] * dot_t(one_b[...], w_second[...])).astype(BF16)
     one_b[...] = dot_t(two_b[...], w_first[...]).astype(BF16)
-    sent[...] = dot(place_far[...], one_b[...]).astype(BF16)
-    keep_sent = pltpu.make_async_copy(sent, hbm_sent, sem.at[4])
-    keep_sent.start()
+    half = low.shape[1]
+    low[...] = dot(place_far[...], one_b[:, :half]).astype(BF16)
+    keep_low = pltpu.make_async_copy(low, hbm_low, sem.at[4])
+    keep_low.start()
+    high[...] = dot(place_far[...], one_b[:, half:]).astype(BF16)
+    keep_high = pltpu.make_async_copy(high, hbm_high, sem.at[1])
+    keep_high.start()
     out[...] = dot(place[...], one_b[...]).astype(BF16)
     keep_out = pltpu.make_async_copy(out, hbm_out, sem.at[0])
     keep_out.start()
     keep_codes.wait()
-    keep_sent.wait()
+    keep_slots.wait()
+    keep_low.wait()
+    keep_high.wait()
     keep_out.wait()
 
 
 def near_adjoint_kernel(
     flip, rest, cells_own, cells_near, codes, near_codes, far_codes, far_slots, courant,
     kept_a, kept_b, kept_c, far_mats, spread,
-    table, mats, cells_b, mid_b, mid_f,
+    table, mats, cells_b, mid_b, mid_f, slots_b, codes_b, sem,
 ):
     rows, lon = 4, table.shape[1]
     cells = rows * lon
+    own_copy = pltpu.make_async_copy(cells_own, cells_b.at[0:cells], sem.at[0])
+    own_copy.start()
+    slots_copy = pltpu.make_async_copy(far_slots, slots_b, sem.at[1])
+    slots_copy.start()
+    codes_copy = pltpu.make_async_copy(far_codes, codes_b, sem.at[2])
+    codes_copy.start()
+    codes_copy.wait()
     sign = sign_of(flip)
-    store_sources(table, 0, far_codes[...], True, sign, lon, rows)
+    store_sources(table, 0, codes_b[...], True, sign, lon, rows)
     store_sources(table, 1, codes[...], False, sign, lon, rows)
     store_sources(table, 2, near_codes[...], True, sign, lon, rows)
     k = 0
@@ -451,11 +463,12 @@
         for ext in exts:
             push_matrix(mats.at[k], table, 3 - order, ext, lon, rows)
             k += 1
-    cells_b[0:cells, :] = cells_own[...]
     for j in range(rows):
         cells_b[(rows + j) * lon : (rows + j + 1) * lon, :] = cells_near[
             (rows - 1 - j) * lon : (rows - j) * lon, :
         ]
+
+    own_copy.wait()
 
     def advect(cs):
         near_steps(
@@ -464,34 +477,42 @@
             (kept_a, kept_b, kept_c), mid_b, mid_f, lon, cs,
         )
 
-    by_parts(cells_own.shape[1], advect)
+    advect(slice(None))
     for order in range(4):
         for half in range(2):
             push_matrix(far_mats.at[2 * order + half], table, 3 - order, order + 1 + 2 * half, lon, rows)
-    where = turn(far_slots[...])
+    slots_copy.wait()
+    where = turn(slots_b[...])
     capacity = spread.shape[1]
     for j in range(rows):
         spread[j * lon : (j + 1) * lon, :] = spread_matrix(where, j, capacity)
 
 
 def far_adjoint_kernel(
-    flip, flag, cells_own, far, rest, courant, kept_a, kept_b, kept_c, mats, spread, far_slots,
+    part, flip, flag, cells_own, far, rest, courant, kept_a, kept_b, kept_c, mats, spread, far_slots, _given,
     out,
-    cells_b, mid_b, mid_f, result, rest_b, sem,
+    cells_b, mid_b, mid_f, result, rest_b, slots_b, sem,
 ):
     rows, lon = out.shape[0], out.shape[1]
     cells = rows * lon
+    width = far.shape[1]
+    cs = slice(part * width, (part + 1) * width)
     for j in range(rows):
         value = dot(spread[j * lon : (j + 1) * lon, :], far[...])
         cells_b[(rows - 1 - j) * lon : (rows - j) * lon, :] = value.astype(BF16)
-    cells_b[cells:, :] = cells_own[0 : 2 * lon, :]
+    cells_b[cells:, :] = cells_own[0 : 2 * lon, cs]
 
     @pl.when(flag[0] > 0)
     def _():
-        copy = pltpu.make_async_copy(rest, rest_b, sem.at[rows])
-        copy.start()
-        copy.wait()
-        where = turn(far_slots[...])
+        fetches = [
+            pltpu.make_async_copy(rest.at[:, cs], rest_b, sem.at[rows]),
+            pltpu.make_async_copy(far_slots, slots_b, sem.at[rows + 1]),
+        ]
+        for copy in fetches:
+            copy.start()
+        for copy in fetches:
+            copy.wait()
+        where = turn(slots_b[...])
         for j in range(rows):
             value = dot(spread_matrix(where, j, rest_b.shape[0], spread.shape[1]), rest_b[...])
             at = slice((rows - 1 - j) * lon, (rows - j) * lon)
@@ -500,17 +521,17 @@
     copies = []
 
     def finish(half, value):
-        for part in range(2):
-            j = 2 * half + part
-            result[j] = value[part * lon : (part + 1) * lon, :]
+        for piece in range(2):
+            j = 2 * half + piece
+            result[j] = value[piece * lon : (piece + 1) * lon, :]
             at = jnp.where(flip[0] == 1, rows - 1 - j, j)
-            copies.append(pltpu.make_async_copy(result.at[j], out.at[at], sem.at[j]))
+            copies.append(pltpu.make_async_copy(result.at[j], out.at[at, :, cs], sem.at[j]))
             copies[-1].start()
 
     far_steps(
         [mats.at[k] for k in range(8)], lambda at, size: cells_b[at : at + size, :],
-        lambda at, size: cells_b[at : at + size, :].astype(F32), courant,
-        (kept_a, kept_b, kept_c), mid_b, mid_f, lon, finish,
+        lambda at, size: cells_b[at : at + size, :].astype(F32), courant.at[:, cs],
+        tuple(kept.at[:, cs] for kept in (kept_a, kept_b, kept_c)), mid_b, mid_f, lon, finish,
     )
     for copy in copies:
         copy.wait()
@@ -625,11 +646,11 @@
             flip, obs_count, tangent, codes, near, c_row, background[0], w_first, w_second, obs_index, obs_quality,
         )
 
-    column_shape = [pltpu.HBM((cells, levels), BF16), pltpu.HBM((FAR_COLUMNS, levels), BF16)]
+    column_shape = [pltpu.HBM((cells, levels), BF16)] + [pltpu.HBM((FAR_COLUMNS, levels // 2), BF16)] * 2
 
     def run_observe(redo, parts, rest):
         slope_one, slope_two, kept_a, kept_b, kept_c, pick, place, place_far = parts[:8]
-        quality, _, own_mats, own_f, own_b = parts[9:]
+        quality, columns_list, own_mats, own_f, own_b = parts[9:]
         rest_specs = [ANY] if redo else []
         body = functools.partial(observe_kernel, redo)
         rest_args = [rest] if redo else []
@@ -644,9 +665,11 @@
 
         return pl.pallas_call(
             kernel,
-            out_shape=column_shape + [pltpu.HBM((head, lon), F32), shape((1,), jnp.int32)],
-            in_specs=[SMEM, SMEM] + [VMEM] * 5 + rest_specs + [VMEM] * 6 + [ANY] * 3 + [VMEM] * 6,
-            out_specs=[HBM] * 3 + [SMEM],
+            out_shape=column_shape
+            + [pltpu.HBM((head, lon), F32), pltpu.HBM((8, lon), F32)]
+            + [shape((1,), jnp.int32)] * 2,
+            in_specs=[SMEM, SMEM] + [VMEM] * 5 + rest_specs + [VMEM] * 6 + [ANY] * 3 + [VMEM] * 7,
+            out_specs=[HBM] * 5 + [SMEM] * 2,
             scratch_shapes=[
                 pltpu.VMEM((lon, lon), F32),
                 pltpu.VMEM((4, 2 * lon, 4 * lon), BF16),
@@ -660,9 +683,11 @@
                 pltpu.VMEM(w_second.shape, BF16),
                 pltpu.VMEM(w_third.shape, BF16),
                 pltpu.VMEM((cells, levels), BF16),
-                pltpu.VMEM((FAR_COLUMNS, levels), BF16),
+                pltpu.VMEM((FAR_COLUMNS, levels // 2), BF16),
+                pltpu.VMEM((FAR_COLUMNS, levels // 2), BF16),
                 pltpu.VMEM((head, lon), F32),
-                pltpu.SemaphoreType.DMA((6,)),
+                pltpu.VMEM((8, lon), F32),
+                pltpu.SemaphoreType.DMA((7,)),
             ]
             + (rest_scratch if redo else []),
             compiler_params=params(),
@@ -670,41 +695,35 @@
         )(
             flip, linked, slots, own_f, own_b, codes, far, *rest_args, c_row,
             slope_one, slope_two, kept_a, kept_b, kept_c, w_first, w_second, w_third,
-            pick, place, place_far, quality, chan_weight.reshape(1, -1), own_mats,
+            pick, place, place_far, quality, chan_weight.reshape(1, -1), own_mats, columns_list,
         )
 
     parts = run_near()
     near_codes, own_slots = parts[8], parts[10]
-    cells_own, sent, far_codes, over = run_observe(False, parts, None)
+    cells_own, low, high, far_codes, far_slots, over, over_columns = run_observe(False, parts, None)
 
     def observe_again():
         rest = send_rest(FAR_CELLS, slots, own, cells - FAR_CELLS, links)
-        return run_observe(True, run_near(), rest)[:2]
+        return run_observe(True, run_near(), rest)[:3]
 
     redone = lax.cond(over[0] > 0, observe_again, lambda: blank(column_shape))
-    cells_own, sent = pl.pallas_call(
+    cells_own, low, high = pl.pallas_call(
         choose_kernel,
         out_shape=column_shape,
-        in_specs=[SMEM] + [HBM] * 4,
-        out_specs=[HBM] * 2,
-        scratch_shapes=[pltpu.SemaphoreType.DMA((2,))],
-        input_output_aliases={1: 0, 2: 1},
+        in_specs=[SMEM] + [HBM] * 6,
+        out_specs=[HBM] * 3,
+        scratch_shapes=[pltpu.SemaphoreType.DMA((3,))],
+        input_output_aliases={1: 0, 2: 1, 3: 2},
         name="choose",
-    )(over, cells_own, sent, *redone)
-
-    columns_far = lax.ppermute(sent, "lat", links)
+    )(over, cells_own, low, high, *redone)
+
+    far_low = lax.ppermute(low, "lat", links)
+    far_high = lax.ppermute(high, "lat", links)
     cells_near = lax.ppermute(cells_own, "lat", pairs)
 
-    far_slots, over = pl.pallas_call(
-        reach_kernel,
-        out_shape=[shape((8, lon), F32), shape((1,), jnp.int32)],
-        in_specs=[SMEM, SMEM, VMEM, VMEM],
-        out_specs=[VMEM, SMEM],
-        name="reach",
-    )(flip, linked, own_slots, far_codes)
     left = cells - FAR_COLUMNS
     rest = lax.cond(
-        over[0] > 0,
+        over_columns[0] > 0,
         lambda: send_rest(FAR_COLUMNS, own_slots, cells_own, left, links),
         lambda: blank([shape((left, levels), BF16)])[0],
     )
@@ -715,39 +734,59 @@
             shape((8, 2 * lon, 4 * lon), BF16),
             shape((cells, FAR_COLUMNS), BF16),
         ],
-        in_specs=[SMEM, ANY] + [VMEM] * 7,
+        in_specs=[SMEM, ANY, ANY] + [VMEM] * 3 + [ANY, ANY, VMEM],
         out_specs=[VMEM] * 5,
         scratch_shapes=[
             pltpu.VMEM((lon, lon), F32),
             pltpu.VMEM((6, 2 * lon, 4 * lon), BF16),
             pltpu.VMEM((2 * cells, levels), BF16),
-            pltpu.VMEM((2, 6 * lon, PART), BF16),
-            pltpu.VMEM((2, 6 * lon, PART), F32),
+            pltpu.VMEM((2, 6 * lon, levels), BF16),
+            pltpu.VMEM((2, 6 * lon, levels), F32),
+            pltpu.VMEM((8, lon), F32),
+            pltpu.VMEM((head, lon), F32),
+            pltpu.SemaphoreType.DMA((3,)),
         ],
         compiler_params=params(),
         cost_estimate=pl.CostEstimate(flops=2_000_000_000, bytes_accessed=8_000_000, transcendentals=0),
         name="near_adjoint",
     )(flip, rest, cells_own, cells_near, codes, near_codes, far_codes, far_slots, c_row)
 
-    return pl.pallas_call(
-        far_adjoint_kernel,
-        out_shape=shape((rows, lon, levels), F32),
-        in_specs=[SMEM, SMEM, VMEM, VMEM, ANY] + [VMEM] * 7,
-        out_specs=HBM,
-        scratch_shapes=[
-            pltpu.VMEM((6 * lon, levels), BF16),
-            pltpu.VMEM((2, 6 * lon, levels), BF16),
-            pltpu.VMEM((2, 6 * lon, levels), F32),
-            pltpu.VMEM((rows, lon, levels), F32),
-            pltpu.VMEM((cells - FAR_COLUMNS, levels), BF16),
-            pltpu.SemaphoreType.DMA((rows + 1,)),
-        ],
-        compiler_params=params(),
-        name="far_adjoint",
-    )(
-        flip, over, cells_own, columns_far, rest, c_row,
-        kept_a, kept_b, kept_c, mats, spread, far_slots,
-    )
+    width = levels // 2
+
+    def finish(part, columns, given):
+        body = functools.partial(far_adjoint_kernel, part)
+        given_specs = [HBM] if part else []
+
+        def kernel(*refs):
+            refs = list(refs)
+            if not part:
+                refs.insert(12, None)
+            body(*refs)
+
+        return pl.pallas_call(
+            kernel,
+            out_shape=shape((rows, lon, levels), F32),
+            in_specs=[SMEM, SMEM, VMEM, VMEM, ANY] + [VMEM] * 6 + [ANY] + given_specs,
+            out_specs=HBM,
+            scratch_shapes=[
+                pltpu.VMEM((6 * lon, width), BF16),
+                pltpu.VMEM((2, 6 * lon, width), BF16),
+                pltpu.VMEM((2, 6 * lon, width), F32),
+                pltpu.VMEM((rows, lon, width), F32),
+                pltpu.VMEM((left, width), BF16),
+                pltpu.VMEM((8, lon), F32),
+                pltpu.SemaphoreType.DMA((rows + 2,)),
+            ],
+            input_output_aliases={12: 0} if part else {},
+            compiler_params=params(),
+            cost_estimate=pl.CostEstimate(flops=2_000_000_000, bytes_accessed=4_000_000, transcendentals=0),
+            name="far_adjoint",
+        )(
+            flip, over_columns, cells_own, columns, rest, c_row, kept_a, kept_b, kept_c, mats, spread, far_slots, *given,
+        )
+
+    half_done = finish(0, far_low, [])
+    return finish(1, far_high, [half_done])
 
 
 def solution(mesh):

time: 60.2 us -> 59.4 us (0.987)
  waiting for transfers between devices: 12.5 us -> 8.75 us
  starting transfers between devices: 5.78 us -> 9.42 us
  local copies, waits for them, and re-layouts: 0.7 us -> 0.03 us
    ppermute x1 -> x2, waiting for transfers between devices: 6.71 us -> 2.94 us  [the longest x1 2.94 us: local(): far_low = lax.ppermute(low, 'lat', links)]
    ppermute x1 -> x2, starting transfers between devices: 1.92 us -> 5.56 us  [the longest x1 3.64 us: local(): far_high = lax.ppermute(high, 'lat', links)]
    pallas_call x1, Pallas kernels: 13.1 us -> 14.2 us  [run_observe(): pl.pallas_call(kernel, out_shape=column_shape + [pltpu.HBM((head, lon), F...]
    pallas_call x1, Pallas kernels: 5.17 us -> 4.25 us  [local(): pl.pallas_call(near_adjoint_kernel, out_shape=kept_shape + [shape((8, 2 *...]
    unnamed x16, local copies, waits for them, and re-layouts: 0.7 us -> 0.03 us
  transfers between devices with their start and end apart: 4 -> 5, of which waited for: 2 -> 2; matrix products, arithmetic and copies ran while one was open for 0% -> 0% of each run, Pallas kernels for 28% -> 29%
where the time goes in v1:
time: 59.4 us; the launch traced here: 59.1 us
  Pallas kernels  38.4 us (65%)
  starting transfers between devices  9.42 us (16%)
  waiting for transfers between devices  8.75 us (15%)
  between operations  2.29 us (4%)
    pallas_call x1, Pallas kernels, run_observe(): pl.pallas_call(kernel, out_shape=column_shape + [pltpu.HBM((head, lon), F...  14.2 us
    pallas_call x1, Pallas kernels, run_near(): pl.pallas_call(near_kernel, out_shape=[slope_shape, slope_shape] + kept_s...  9.54 us
    pallas_call x2, Pallas kernels, finish(): pl.pallas_call(kernel, out_shape=shape((rows, lon, levels), F32), in_spec...  6.61 us
    ppermute x1, waiting for transfers between devices, local(): far = lax.ppermute(sent, 'lat', links)  5.81 us
    pallas_call x1, Pallas kernels, local(): pl.pallas_call(near_adjoint_kernel, out_shape=kept_shape + [shape((8, 2 *...  4.25 us
    ppermute x1, starting transfers between devices, local(): far_high = lax.ppermute(high, 'lat', links)  3.64 us
    pallas_call x1, Pallas kernels, local(): pl.pallas_call(pack_kernel, out_shape=[shape((cells + head, levels), BF16...  3.13 us
    ppermute x1, starting transfers between devices, local(): far = lax.ppermute(sent, 'lat', links)  3.05 us
  transfers between devices with their start and end apart: 5, of which 2 were waited for; matrix products, arithmetic and copies ran while one was open for 0% of the time, Pallas kernels for 29%

profile of v1, /device:TPU:25, one launch (start us, length us, event | category | flops | bytes accessed | tf_op | source)
XLA Modules:
  0.0 59.1 jit_solution(1908490732838195659)
XLA Ops:
  0.0 0.0 copy-start.3
  0.0 0.0 copy-start.4
  0.0 0.0 copy-start.6
  0.0 0.0 copy-start.7
  0.0 3.1 %pack.1 = (bf16[528,1024]{1,0:T(8,128)(2,1)}, bf16[320,1024]{1,0:T(8,128)(2,1)}, f32[16,128]{1,0:T(8,128)S(1)}, f32[8,128]{1,0:T(8,128)S(1)}) custom-call(s32[1]{0:T(128)} %bitcast.2.flip.refs_0_, f32[4,128,1024]{2,1,0:T(8,128)} %tangent.3, s32[4,4,128]{2,1,0:T(4,128)} %wind.1), custom_call_target="tpu_custom_call" | custom-call | tf_op jit(solution)/shard_map/pack/pallas_call | solution.py:590
  3.2 0.7 %collective-permute-start.2 = (bf16[528,1024]{1,0:T(8,128)(2,1)}, bf16[528,1024]{1,0:T(8,128)(2,1)}, u32[]{:S(2)}, u32[]{:S(2)}) collective-permute-start(bf16[528,1024]{1,0:T(8,128)(2,1)} %get-tuple-element.119), channel_id=1, source_target_pairs={{0,1},{1,0},{2,3},{3,2},{4,5},{5,4},{6,7},{7,6},{8,9},{9,8},{10,11... | collective-permute-start | bytes 3244040 | tf_op jit(solution)/shard_map/ppermute | solution.py:610
  3.9 3.0 %collective-permute-start.3 = (bf16[320,1024]{1,0:T(8,128)(2,1)}, bf16[320,1024]{1,0:T(8,128)(2,1)S(1)}, u32[]{:S(2)}, u32[]{:S(2)}) collective-permute-start(bf16[320,1024]{1,0:T(8,128)(2,1)} %get-tuple-element.122), channel_id=1, source_target_pairs={{1,2},{3,4},{5,6},{7,8},{9,10},{11,12},{13,14},{2,1},{4,3},{6,5},{... | collective-permute-start | bytes 1966088 | tf_op jit(solution)/shard_map/ppermute | solution.py:609
  7.6 0.0 collective-permute-done.2.near
  7.6 0.0 copy-done.3
  7.6 0.0 copy-done.4
  7.7 0.0 copy-done.6
  7.7 0.0 copy-done.7
  7.7 0.0 copy-start.5
  7.7 9.5 %near.3 = (f32[480,1024]{1,0:T(8,128)S(1)}, f32[480,1024]{1,0:T(8,128)S(1)}, f32[256,1024]{1,0:T(8,128)S(1)}, f32[256,1024]{1,0:T(8,128)S(1)}, f32[256,1024]{1,0...) custom-call(s32[1]{0:T(128)} %bitcast.2.flip.refs_0_, ...), custom_call_target="tpu_custom_call" | custom-call | flops 4000000000 | bytes 16000000 | tf_op jit(solution)/shard_map/near/pallas_call | solution.py:617
  17.2 5.8 %collective-permute-done.3.refs_6_ = bf16[320,1024]{1,0:T(8,128)(2,1)S(1)} collective-permute-done((bf16[320,1024]{1,0:T(8,128)(2,1)}, bf16[320,1024]{1,0:T(8,128)(2,1)S(1)}, u32[]{:S(2)}, u32[]{:S(2)}) %collective-permute-start.3) | collective-permute-done | bytes 655392 | tf_op jit(solution)/shard_map/ppermute | solution.py:609
  23.0 0.0 copy-done.5
  23.0 14.2 %observe.3 = (bf16[512,1024]{1,0:T(8,128)(2,1)}, bf16[256,512]{1,0:T(8,128)(2,1)}, bf16[256,512]{1,0:T(8,128)(2,1)}, f32[16,128]{1,0:T(8,128)}, f32[8,128]{1,0:T(8,128)}, /*index=5*/s32[1]{0:T(128)}, s32[1]{0:T(128)}) custom-call(s32[1]{0:T(128)} %bitcast.2.flip.refs_0_, s32[1]{0:T(128)} %bitcast.3.refs_1_, f32[8,128]{1,0:T(8,128)S(1)} %get-tuple-element.117.refs_2_, ...), custom_call_target="tpu_custom_call" | custom-call | tf_op jit(solution)/shard_map/observe/pallas_call | solution.py:666
  37.8 0.2 conditional.2
  38.1 0.0 copy-start
  38.1 0.0 copy-start.1
  38.1 0.6 %choose.1 = (bf16[512,1024]{1,0:T(8,128)(2,1)}, bf16[256,512]{1,0:T(8,128)(2,1)}, bf16[256,512]{1,0:T(8,128)(2,1)}) custom-call(s32[1]{0:T(128)} %get-tuple-element.135.flag, bf16[512,1024]{1,0:T(8,128)(2,1)} %get-tuple-element.136.refs_0_, bf16[256,512]{1,0:T(8,128)(2,1)} %get-tuple-element.137.refs_1_, ...), custom_call_target="tpu_custom_call", output_to_operand_aliasing={{0}: (1, {}), {1}: (2, {}), {2}: (3, {})} | custom-call | tf_op jit(solution)/shard_map/choose/pallas_call | solution.py:710
  38.7 0.1 collective-permute-start.5
  38.8 1.9 %collective-permute-start.6 = (bf16[256,512]{1,0:T(8,128)(2,1)}, bf16[256,512]{1,0:T(8,128)(2,1)S(1)}, u32[]{:S(2)}, u32[]{:S(2)}) collective-permute-start(bf16[256,512]{1,0:T(8,128)(2,1)} %get-tuple-element.152), channel_id=1, source_target_pairs={{1,2},{3,4},{5,6},{7,8},{9,10},{11,12},{13,14},{2,1},{4,3},{6,5},{... | collective-permute-start | bytes 786440 | tf_op jit(solution)/shard_map/ppermute | solution.py:720
  41.4 3.6 %collective-permute-start.4 = (bf16[256,512]{1,0:T(8,128)(2,1)}, bf16[256,512]{1,0:T(8,128)(2,1)S(1)}, u32[]{:S(2)}, u32[]{:S(2)}) collective-permute-start(bf16[256,512]{1,0:T(8,128)(2,1)} %get-tuple-element.143), channel_id=1, source_target_pairs={{1,2},{3,4},{5,6},{7,8},{9,10},{11,12},{13,14},{2,1},{4,3},{6,5},{... | collective-permute-start | bytes 786440 | tf_op jit(solution)/shard_map/ppermute | solution.py:721
  45.1 0.0 collective-permute-done.5.cells_near
  45.1 0.0 copy-done
  45.1 0.0 copy-done.1
  45.1 0.0 copy-start.2
  45.1 4.3 %near_adjoint.1 = (f32[256,1024]{1,0:T(8,128)S(1)}, f32[256,1024]{1,0:T(8,128)S(1)}, f32[256,1024]{1,0:T(8,128)S(1)}, bf16[8,256,512]{2,1,0:T(8,128)(2,1)S(1)}, bf16[512,256]{1,0:T(8,128)(2,1)S(1)}) custom-call(s32[1]{0:T(128)} %bitcast.2.flip.refs_0_, bf16[256,1024]{1,0:T(8,128)(2,1)} %get-tuple-element.160.rest.refs_4_, ...), custom_call_target="tpu_custom_call" | custom-call | flops 2000000000 | bytes 8000000 | tf_op jit(solution)/shard_map/near_adjoint/pallas_call | solution.py:730
  49.4 2.9 %collective-permute-done.6.refs_3_ = bf16[256,512]{1,0:T(8,128)(2,1)S(1)} collective-permute-done((bf16[256,512]{1,0:T(8,128)(2,1)}, bf16[256,512]{1,0:T(8,128)(2,1)S(1)}, u32[]{:S(2)}, u32[]{:S(2)}) %collective-permute-start.6) | collective-permute-done | bytes 262176 | tf_op jit(solution)/shard_map/ppermute | solution.py:720
  52.3 0.0 copy-done.2
  52.3 3.3 %far_adjoint.2.refs_12_ = f32[4,128,1024]{2,1,0:T(8,128)} custom-call(s32[1]{0:T(128)} %bitcast.2.flip.refs_0_, s32[1]{0:T(128)} %get-tuple-element.134.refs_1_, bf16[512,1024]{1,0:T(8,128)(2,1)S(1)} %copy-done.2, bf16[256,512]{1,0:T(8,128)(2,1)S(1)} %collective-permute-done.6.refs_3_, bf16[256,1024]{1,0:T(8,128)(2,1)} %get-tuple-element.160.rest.refs_4_, ...), custom_call_target="tpu_custom_call" | custom-call | flops 2000000000 | bytes 4000000 | tf_op jit(solution)/shard_map/far_adjoint/pallas_call | solution.py:766
  55.6 0.0 collective-permute-done.4.refs_3_
  55.6 3.3 %far_adjoint.3 = f32[4,128,1024]{2,1,0:T(8,128)} custom-call(s32[1]{0:T(128)} %bitcast.2.flip.refs_0_, s32[1]{0:T(128)} %get-tuple-element.134.refs_1_, bf16[512,1024]{1,0:T(8,128)(2,1)S(1)} %copy-done.2, bf16[256,512]{1,0:T(8,128)(2,1)S(1)} %collective-permute-done.4.refs_3_, ...), custom_call_target="tpu_custom_call", output_to_operand_aliasing={{}: (12, {})} | custom-call | flops 2000000000 | bytes 4000000 | tf_op jit(solution)/shard_map/far_adjoint/pallas_call | solution.py:766
  (3 shorter events, 0.0 us)
Async XLA Ops:
  0.0 7.6 %copy-start.3 = (f32[4,128,1024]{2,1,0:T(8,128)S(1)}, f32[4,128,1024]{2,1,0:T(8,128)}, u32[]{:S(2)}) copy-start(f32[4,128,1024]{2,1,0:T(8,128)} %tangent.3) | copy-start | bytes 6291460
  0.0 7.6 %copy-start.4 = (f32[1024]{0:T(1024)S(1)}, f32[1024]{0:T(1024)}, u32[]{:S(2)}) copy-start(f32[1024]{0:T(1024)} %param.17) | copy-start | bytes 12292
  0.0 7.6 %copy-start.6 = (s32[1,480]{1,0:T(1,128)S(1)}, s32[1,480]{1,0:T(1,128)}, u32[]{:S(2)}) copy-start(s32[1,480]{1,0:T(1,128)} %obs_index.1) | copy-start | bytes 5764
  0.0 7.7 %copy-start.7 = (bf16[1,480]{1,0:T(2,128)(2,1)S(1)}, bf16[1,480]{1,0:T(2,128)(2,1)}, u32[]{:S(2)}) copy-start(bf16[1,480]{1,0:T(2,128)(2,1)} %obs_quality.1) | copy-start | bytes 2884
  3.2 4.5 %collective-permute-start.2 = (bf16[528,1024]{1,0:T(8,128)(2,1)}, bf16[528,1024]{1,0:T(8,128)(2,1)}, u32[]{:S(2)}, u32[]{:S(2)}) collective-permute-start(bf16[528,1024]{1,0:T(8,128)(2,1)} %get-tuple-element.119), channel_id=1, source_target_pairs={{0,1},{1,0},{2,3},{3,2},{4,5},{5,4},{6,7},{7,6},{8,9},{9,8},{10,11... | collective-permute-start | bytes 3244040 | tf_op jit(solution)/shard_map/ppermute | solution.py:610
  3.9 19.1 %collective-permute-start.3 = (bf16[320,1024]{1,0:T(8,128)(2,1)}, bf16[320,1024]{1,0:T(8,128)(2,1)S(1)}, u32[]{:S(2)}, u32[]{:S(2)}) collective-permute-start(bf16[320,1024]{1,0:T(8,128)(2,1)} %get-tuple-element.122), channel_id=1, source_target_pairs={{1,2},{3,4},{5,6},{7,8},{9,10},{11,12},{13,14},{2,1},{4,3},{6,5},{... | collective-permute-start | bytes 1966088 | tf_op jit(solution)/shard_map/ppermute | solution.py:609
  7.7 15.4 %copy-start.5 = (f32[1024]{0:T(1024)S(1)}, f32[1024]{0:T(1024)}, u32[]{:S(2)}) copy-start(f32[1024]{0:T(1024)} %param.25) | copy-start | bytes 12292
  38.1 7.0 %copy-start = (f32[8,128]{1,0:T(8,128)S(1)}, f32[8,128]{1,0:T(8,128)}, u32[]{:S(2)}) copy-start(f32[8,128]{1,0:T(8,128)} %get-tuple-element.146.far_slots.refs_11_) | copy-start | bytes 12292
  38.1 7.0 %copy-start.1 = (f32[16,128]{1,0:T(8,128)S(1)}, f32[16,128]{1,0:T(8,128)}, u32[]{:S(2)}) copy-start(f32[16,128]{1,0:T(8,128)} %get-tuple-element.145.far_codes) | copy-start | bytes 24580
  38.7 6.4 %collective-permute-start.5 = (bf16[512,1024]{1,0:T(8,128)(2,1)}, bf16[512,1024]{1,0:T(8,128)(2,1)S(1)}, u32[]{:S(2)}, u32[]{:S(2)}) collective-permute-start(bf16[512,1024]{1,0:T(8,128)(2,1)} %get-tuple-element.142.cells_own.refs_2_), channel_id=1, source_target_pairs={{0,1},{1,0},{2,3},{3,2},{4,5},{5,4},{6,7},{7,6},{8,9},{9,8},{10,11... | collective-permute-start | bytes 3145736 | tf_op jit(solution)/shard_map/ppermute | solution.py:722
  38.8 13.5 %collective-permute-start.6 = (bf16[256,512]{1,0:T(8,128)(2,1)}, bf16[256,512]{1,0:T(8,128)(2,1)S(1)}, u32[]{:S(2)}, u32[]{:S(2)}) collective-permute-start(bf16[256,512]{1,0:T(8,128)(2,1)} %get-tuple-element.152), channel_id=1, source_target_pairs={{1,2},{3,4},{5,6},{7,8},{9,10},{11,12},{13,14},{2,1},{4,3},{6,5},{... | collective-permute-start | bytes 786440 | tf_op jit(solution)/shard_map/ppermute | solution.py:720
  41.4 14.2 %collective-permute-start.4 = (bf16[256,512]{1,0:T(8,128)(2,1)}, bf16[256,512]{1,0:T(8,128)(2,1)S(1)}, u32[]{:S(2)}, u32[]{:S(2)}) collective-permute-start(bf16[256,512]{1,0:T(8,128)(2,1)} %get-tuple-element.143), channel_id=1, source_target_pairs={{1,2},{3,4},{5,6},{7,8},{9,10},{11,12},{13,14},{2,1},{4,3},{6,5},{... | collective-permute-start | bytes 786440 | tf_op jit(solution)/shard_map/ppermute | solution.py:721
  45.1 7.2 %copy-start.2 = (bf16[512,1024]{1,0:T(8,128)(2,1)S(1)}, bf16[512,1024]{1,0:T(8,128)(2,1)}, u32[]{:S(2)}) copy-start(bf16[512,1024]{1,0:T(8,128)(2,1)} %get-tuple-element.142.cells_own.refs_2_) | copy-start | bytes 3145732

commit v2 on v1

--- a/solution.py
+++ b/solution.py
@@ -10,7 +10,8 @@
 F32 = jnp.float32
 BF16 = jnp.bfloat16
 PART = 512
-FAR_CELLS = 304
+NOTE_ROWS = 8
+FAR_CELLS = 296
 FAR_COLUMNS = 256
 ANY = pl.BlockSpec(memory_space=pl.ANY)
 VMEM = pl.BlockSpec(memory_space=pltpu.VMEM)
@@ -174,18 +175,19 @@
     where, total = slot_of(mask)
     slots[...] = where
     head = codes.shape[0]
-    capacity = sent.shape[0] - head
-    tall = jnp.concatenate([mask, jnp.zeros((head - mask.shape[0], lon), F32)], axis=0)
-    flag = jnp.broadcast_to(jnp.where(total > float(capacity), 1.0, 0.0), (head, lon))
-    notes = jnp.concatenate([codes[...], tall, flag, jnp.zeros((head, own.shape[1] - 3 * lon), F32)], axis=1)
-    notes = notes.astype(BF16)
-    own[cells:, :] = notes
-    sent[capacity:, :] = notes
-    choose = choose_matrix(where, capacity, rows)
+    flag = jnp.broadcast_to(jnp.where(total > float(FAR_CELLS), 1.0, 0.0), (NOTE_ROWS, lon))
+    blank_lanes = own.shape[1] - lon
+    own[cells:, :] = jnp.concatenate([codes[...], jnp.zeros((head, blank_lanes), F32)], axis=1).astype(BF16)
+    notes = [codes[0:NOTE_ROWS], codes[NOTE_ROWS:], mask, flag, jnp.zeros((NOTE_ROWS, blank_lanes - 3 * lon), F32)]
+    choose = choose_matrix(where, sent.shape[0], rows)
     for j in range(rows):
         copies[j].wait()
         own[j * lon : (j + 1) * lon, :] = buf[j].astype(BF16)
-    sent[0:capacity, :] = dot(choose, own[0:cells, :]).astype(BF16)
+    chosen = dot(choose, own[0:cells, :])
+    last = FAR_CELLS - NOTE_ROWS
+    sent[0:last, :] = chosen[0:last].astype(BF16)
+    tail = jnp.concatenate([chosen[last:FAR_CELLS], jnp.concatenate(notes, axis=1)], axis=0)
+    sent[last:, :] = tail.astype(BF16)
 
 
 def choose_kernel(flag, *refs):
@@ -255,13 +257,16 @@
             value = (1.0 - c) * own + c * dot(mats[k][...], window)
             k += 1
             if step < 3:
-                mid_f[now, at : at + 2 * lon, :] = value
+                if half == 0:
+                    mid_f[now, lon : 2 * lon, :] = value[lon:]
+                else:
+                    mid_f[now, at : at + 2 * lon, :] = value
                 mid_b[now, at : at + 2 * lon, :] = value.astype(BF16)
             else:
                 finish(half, value)
         if step < 3:
             carried = kept[step][...]
-            mid_f[now, 4 * lon :, :] = carried
+            mid_f[now, 4 * lon : 5 * lon, :] = carried[0:lon]
             mid_b[now, 4 * lon :, :] = carried.astype(BF16)
 
 
@@ -351,7 +356,6 @@
     rows, lon = 4, own_f.shape[0]
     cells = rows * lon
     sign = sign_of(flip)
-    capacity = far.shape[0] - codes.shape[0]
     loads = [
         pltpu.make_async_copy(hbm_first, w_first, sem.at[0]),
         pltpu.make_async_copy(hbm_second, w_second, sem.at[1]),
@@ -360,7 +364,9 @@
     for copy in loads:
         copy.start()
     table[...] = jnp.zeros_like(table)
-    far_codes[...] = far[capacity:, 0:lon].astype(F32)
+    tail = far[FAR_CELLS - NOTE_ROWS :, 0 : 4 * lon].astype(F32)[NOTE_ROWS:]
+    far_codes[0:NOTE_ROWS, :] = tail[:, 0:lon]
+    far_codes[NOTE_ROWS:, :] = tail[:, lon : 2 * lon]
     store_sources(table, 0, far_codes[...], True, sign, lon, rows)
     store_sources(table, 1, codes[...], False, sign, lon, rows)
     turned = table[...].T
@@ -378,12 +384,12 @@
     for k, (step, half) in enumerate(FAR_BLOCKS):
         pull_matrix(mats.at[k], turned, step, step + 1 + 2 * half, lon, rows)
         chosen[2 * step + half] = mats.at[k]
-    where, _ = slot_of(far[capacity:, lon : 2 * lon].astype(F32)[0:8])
-    where = turn(where)
-    most = jnp.maximum(jnp.max(far[capacity:, 2 * lon : 3 * lon].astype(F32)), jnp.where(jnp.max(slots[...]) >= float(capacity), 1.0, 0.0))
+    listed, _ = slot_of(tail[:, 2 * lon : 3 * lon])
+    where = turn(jnp.where(listed < float(FAR_CELLS), listed, -1.0))
+    most = jnp.maximum(jnp.max(tail[:, 3 * lon :]), jnp.where(jnp.max(slots[...]) >= float(FAR_CELLS), 1.0, 0.0))
     over[0] = jnp.where(most > 0.0, linked[0], 0)
     for j in range(rows):
-        value = dot(spread_matrix(where, j, capacity), far[0:capacity, :])
+        value = dot(spread_matrix(where, j, far.shape[0]), far[...])
         cells_b[(rows - 1 - j) * lon : (rows - j) * lon, :] = value.astype(BF16)
     cells_b[cells:, :] = own_b[...]
 
@@ -391,8 +397,9 @@
         copy = pltpu.make_async_copy(rest, rest_b, sem.at[5])
         copy.start()
         copy.wait()
+        where = turn(jnp.where(listed < float(FAR_CELLS), -1.0, listed))
         for j in range(rows):
-            value = dot(spread_matrix(where, j, rest_b.shape[0], capacity), rest_b[...])
+            value = dot(spread_matrix(where, j, rest_b.shape[0], FAR_CELLS - NOTE_ROWS), rest_b[...])
             at = slice((rows - 1 - j) * lon, (rows - j) * lon)
             cells_b[at, :] = (cells_b[at, :].astype(F32) + value).astype(BF16)
 
@@ -591,7 +598,7 @@
         pack_kernel,
         out_shape=[
             shape((cells + head, levels), BF16),
-            shape((FAR_CELLS + head, levels), BF16),
+            shape((FAR_CELLS + NOTE_ROWS, levels), BF16),
             shape((head, lon), F32),
             shape((8, lon), F32),
         ],
@@ -654,7 +661,7 @@
         rest_specs = [ANY] if redo else []
         body = functools.partial(observe_kernel, redo)
         rest_args = [rest] if redo else []
-        rest_scratch = [pltpu.VMEM((cells - FAR_CELLS, levels), BF16)]
+        rest_scratch = [pltpu.VMEM((cells - FAR_CELLS + NOTE_ROWS, levels), BF16)]
 
         def kernel(*refs):
             refs = list(refs)
@@ -703,7 +710,8 @@
     cells_own, low, high, far_codes, far_slots, over, over_columns = run_observe(False, parts, None)
 
     def observe_again():
-        rest = send_rest(FAR_CELLS, slots, own, cells - FAR_CELLS, links)
+        first = FAR_CELLS - NOTE_ROWS
+        rest = send_rest(first, slots, own, cells - first, links)
         return run_observe(True, run_near(), rest)[:3]
 
     redone = lax.cond(over[0] > 0, observe_again, lambda: blank(column_shape))

time: 59.4 us -> 58.7 us (0.988)
  waiting for transfers between devices: 8.75 us -> 8.05 us
    ppermute x1, waiting for transfers between devices: 5.81 us -> 5.11 us  [local(): far = lax.ppermute(sent, 'lat', links)]
where the time goes in v2:
time: 58.7 us; the launch traced here: 58.4 us
  Pallas kernels  38.4 us (65%)
  starting transfers between devices  9.42 us (16%)
  waiting for transfers between devices  8.05 us (14%)
  between operations  2.29 us (4%)
    pallas_call x1, Pallas kernels, run_observe(): pl.pallas_call(kernel, out_shape=column_shape + [pltpu.HBM((head, lon), F...  14.2 us
    pallas_call x1, Pallas kernels, run_near(): pl.pallas_call(near_kernel, out_shape=[slope_shape, slope_shape] + kept_s...  9.54 us
    pallas_call x2, Pallas kernels, finish(): pl.pallas_call(kernel, out_shape=shape((rows, lon, levels), F32), in_spec...  6.62 us
    ppermute x1, waiting for transfers between devices, local(): far = lax.ppermute(sent, 'lat', links)  5.11 us
    pallas_call x1, Pallas kernels, local(): pl.pallas_call(near_adjoint_kernel, out_shape=kept_shape + [shape((8, 2 *...  4.25 us
    ppermute x1, starting transfers between devices, local(): far_high = lax.ppermute(high, 'lat', links)  3.64 us
    pallas_call x1, Pallas kernels, local(): pl.pallas_call(pack_kernel, out_shape=[shape((cells + head, levels), BF16...  3.13 us
    ppermute x1, starting transfers between devices, local(): far = lax.ppermute(sent, 'lat', links)  3.05 us
  transfers between devices with their start and end apart: 5, of which 2 were waited for; matrix products, arithmetic and copies ran while one was open for 0% of the time, Pallas kernels for 29%

profile of v2, /device:TPU:25, one launch (start us, length us, event | category | flops | bytes accessed | tf_op | source)
XLA Modules:
  0.0 58.4 jit_solution(12337404921718410368)
XLA Ops:
  0.0 0.0 copy-start.3
  0.0 0.0 copy-start.4
  0.0 0.0 copy-start.6
  0.0 0.0 copy-start.7
  0.0 3.1 %pack.1 = (bf16[528,1024]{1,0:T(8,128)(2,1)}, bf16[304,1024]{1,0:T(8,128)(2,1)}, f32[16,128]{1,0:T(8,128)S(1)}, f32[8,128]{1,0:T(8,128)S(1)}) custom-call(s32[1]{0:T(128)} %bitcast.2.flip.refs_0_, f32[4,128,1024]{2,1,0:T(8,128)} %tangent.3, s32[4,4,128]{2,1,0:T(4,128)} %wind.1), custom_call_target="tpu_custom_call" | custom-call | tf_op jit(solution)/shard_map/pack/pallas_call | solution.py:597
  3.2 0.7 %collective-permute-start.2 = (bf16[528,1024]{1,0:T(8,128)(2,1)}, bf16[528,1024]{1,0:T(8,128)(2,1)}, u32[]{:S(2)}, u32[]{:S(2)}) collective-permute-start(bf16[528,1024]{1,0:T(8,128)(2,1)} %get-tuple-element.119), channel_id=1, source_target_pairs={{0,1},{1,0},{2,3},{3,2},{4,5},{5,4},{6,7},{7,6},{8,9},{9,8},{10,11... | collective-permute-start | bytes 3244040 | tf_op jit(solution)/shard_map/ppermute | solution.py:617
  3.9 3.0 %collective-permute-start.3 = (bf16[304,1024]{1,0:T(8,128)(2,1)}, bf16[304,1024]{1,0:T(8,128)(2,1)S(1)}, u32[]{:S(2)}, u32[]{:S(2)}) collective-permute-start(bf16[304,1024]{1,0:T(8,128)(2,1)} %get-tuple-element.122), channel_id=1, source_target_pairs={{1,2},{3,4},{5,6},{7,8},{9,10},{11,12},{13,14},{2,1},{4,3},{6,5},{... | collective-permute-start | bytes 1867784 | tf_op jit(solution)/shard_map/ppermute | solution.py:616
  7.6 0.0 collective-permute-done.2.near
  7.6 0.0 copy-done.3
  7.6 0.0 copy-done.4
  7.7 0.0 copy-done.6
  7.7 0.0 copy-done.7
  7.7 0.0 copy-start.5
  7.7 9.5 %near.3 = (f32[480,1024]{1,0:T(8,128)S(1)}, f32[480,1024]{1,0:T(8,128)S(1)}, f32[256,1024]{1,0:T(8,128)S(1)}, f32[256,1024]{1,0:T(8,128)S(1)}, f32[256,1024]{1,0...) custom-call(s32[1]{0:T(128)} %bitcast.2.flip.refs_0_, ...), custom_call_target="tpu_custom_call" | custom-call | flops 4000000000 | bytes 16000000 | tf_op jit(solution)/shard_map/near/pallas_call | solution.py:624
  17.2 5.1 %collective-permute-done.3.refs_6_ = bf16[304,1024]{1,0:T(8,128)(2,1)S(1)} collective-permute-done((bf16[304,1024]{1,0:T(8,128)(2,1)}, bf16[304,1024]{1,0:T(8,128)(2,1)S(1)}, u32[]{:S(2)}, u32[]{:S(2)}) %collective-permute-start.3) | collective-permute-done | bytes 622624 | tf_op jit(solution)/shard_map/ppermute | solution.py:616
  22.3 0.0 copy-done.5
  22.3 14.2 %observe.3 = (bf16[512,1024]{1,0:T(8,128)(2,1)}, bf16[256,512]{1,0:T(8,128)(2,1)}, bf16[256,512]{1,0:T(8,128)(2,1)}, f32[16,128]{1,0:T(8,128)}, f32[8,128]{1,0:T(8,128)}, /*index=5*/s32[1]{0:T(128)}, s32[1]{0:T(128)}) custom-call(s32[1]{0:T(128)} %bitcast.2.flip.refs_0_, s32[1]{0:T(128)} %bitcast.3.refs_1_, f32[8,128]{1,0:T(8,128)S(1)} %get-tuple-element.117.refs_2_, ...), custom_call_target="tpu_custom_call" | custom-call | tf_op jit(solution)/shard_map/observe/pallas_call | solution.py:673
  37.1 0.2 conditional.2
  37.4 0.0 copy-start
  37.4 0.0 copy-start.1
  37.4 0.6 %choose.1 = (bf16[512,1024]{1,0:T(8,128)(2,1)}, bf16[256,512]{1,0:T(8,128)(2,1)}, bf16[256,512]{1,0:T(8,128)(2,1)}) custom-call(s32[1]{0:T(128)} %get-tuple-element.135.flag, bf16[512,1024]{1,0:T(8,128)(2,1)} %get-tuple-element.136.refs_0_, bf16[256,512]{1,0:T(8,128)(2,1)} %get-tuple-element.137.refs_1_, ...), custom_call_target="tpu_custom_call", output_to_operand_aliasing={{0}: (1, {}), {1}: (2, {}), {2}: (3, {})} | custom-call | tf_op jit(solution)/shard_map/choose/pallas_call | solution.py:718
  38.0 0.1 collective-permute-start.5
  38.1 1.9 %collective-permute-start.6 = (bf16[256,512]{1,0:T(8,128)(2,1)}, bf16[256,512]{1,0:T(8,128)(2,1)S(1)}, u32[]{:S(2)}, u32[]{:S(2)}) collective-permute-start(bf16[256,512]{1,0:T(8,128)(2,1)} %get-tuple-element.152), channel_id=1, source_target_pairs={{1,2},{3,4},{5,6},{7,8},{9,10},{11,12},{13,14},{2,1},{4,3},{6,5},{... | collective-permute-start | bytes 786440 | tf_op jit(solution)/shard_map/ppermute | solution.py:728
  40.7 3.6 %collective-permute-start.4 = (bf16[256,512]{1,0:T(8,128)(2,1)}, bf16[256,512]{1,0:T(8,128)(2,1)S(1)}, u32[]{:S(2)}, u32[]{:S(2)}) collective-permute-start(bf16[256,512]{1,0:T(8,128)(2,1)} %get-tuple-element.143), channel_id=1, source_target_pairs={{1,2},{3,4},{5,6},{7,8},{9,10},{11,12},{13,14},{2,1},{4,3},{6,5},{... | collective-permute-start | bytes 786440 | tf_op jit(solution)/shard_map/ppermute | solution.py:729
  44.4 0.0 collective-permute-done.5.cells_near
  44.4 0.0 copy-done
  44.4 0.0 copy-done.1
  44.4 0.0 copy-start.2
  44.4 4.3 %near_adjoint.1 = (f32[256,1024]{1,0:T(8,128)S(1)}, f32[256,1024]{1,0:T(8,128)S(1)}, f32[256,1024]{1,0:T(8,128)S(1)}, bf16[8,256,512]{2,1,0:T(8,128)(2,1)S(1)}, bf16[512,256]{1,0:T(8,128)(2,1)S(1)}) custom-call(s32[1]{0:T(128)} %bitcast.2.flip.refs_0_, bf16[256,1024]{1,0:T(8,128)(2,1)} %get-tuple-element.160.rest.refs_4_, ...), custom_call_target="tpu_custom_call" | custom-call | flops 2000000000 | bytes 8000000 | tf_op jit(solution)/shard_map/near_adjoint/pallas_call | solution.py:738
  48.7 2.9 %collective-permute-done.6.refs_3_ = bf16[256,512]{1,0:T(8,128)(2,1)S(1)} collective-permute-done((bf16[256,512]{1,0:T(8,128)(2,1)}, bf16[256,512]{1,0:T(8,128)(2,1)S(1)}, u32[]{:S(2)}, u32[]{:S(2)}) %collective-permute-start.6) | collective-permute-done | bytes 262176 | tf_op jit(solution)/shard_map/ppermute | solution.py:728
  51.6 0.0 copy-done.2
  51.6 3.3 %far_adjoint.2.refs_12_ = f32[4,128,1024]{2,1,0:T(8,128)} custom-call(s32[1]{0:T(128)} %bitcast.2.flip.refs_0_, s32[1]{0:T(128)} %get-tuple-element.134.refs_1_, bf16[512,1024]{1,0:T(8,128)(2,1)S(1)} %copy-done.2, bf16[256,512]{1,0:T(8,128)(2,1)S(1)} %collective-permute-done.6.refs_3_, bf16[256,1024]{1,0:T(8,128)(2,1)} %get-tuple-element.160.rest.refs_4_, ...), custom_call_target="tpu_custom_call" | custom-call | flops 2000000000 | bytes 4000000 | tf_op jit(solution)/shard_map/far_adjoint/pallas_call | solution.py:774
  54.9 0.0 collective-permute-done.4.refs_3_
  54.9 3.3 %far_adjoint.3 = f32[4,128,1024]{2,1,0:T(8,128)} custom-call(s32[1]{0:T(128)} %bitcast.2.flip.refs_0_, s32[1]{0:T(128)} %get-tuple-element.134.refs_1_, bf16[512,1024]{1,0:T(8,128)(2,1)S(1)} %copy-done.2, bf16[256,512]{1,0:T(8,128)(2,1)S(1)} %collective-permute-done.4.refs_3_, ...), custom_call_target="tpu_custom_call", output_to_operand_aliasing={{}: (12, {})} | custom-call | flops 2000000000 | bytes 4000000 | tf_op jit(solution)/shard_map/far_adjoint/pallas_call | solution.py:774
  (3 shorter events, 0.0 us)
Async XLA Ops:
  0.0 7.6 %copy-start.3 = (f32[4,128,1024]{2,1,0:T(8,128)S(1)}, f32[4,128,1024]{2,1,0:T(8,128)}, u32[]{:S(2)}) copy-start(f32[4,128,1024]{2,1,0:T(8,128)} %tangent.3) | copy-start | bytes 6291460
  0.0 7.6 %copy-start.4 = (f32[1024]{0:T(1024)S(1)}, f32[1024]{0:T(1024)}, u32[]{:S(2)}) copy-start(f32[1024]{0:T(1024)} %param.17) | copy-start | bytes 12292
  0.0 7.6 %copy-start.6 = (s32[1,480]{1,0:T(1,128)S(1)}, s32[1,480]{1,0:T(1,128)}, u32[]{:S(2)}) copy-start(s32[1,480]{1,0:T(1,128)} %obs_index.1) | copy-start | bytes 5764
  0.0 7.7 %copy-start.7 = (bf16[1,480]{1,0:T(2,128)(2,1)S(1)}, bf16[1,480]{1,0:T(2,128)(2,1)}, u32[]{:S(2)}) copy-start(bf16[1,480]{1,0:T(2,128)(2,1)} %obs_quality.1) | copy-start | bytes 2884
  3.2 4.5 %collective-permute-start.2 = (bf16[528,1024]{1,0:T(8,128)(2,1)}, bf16[528,1024]{1,0:T(8,128)(2,1)}, u32[]{:S(2)}, u32[]{:S(2)}) collective-permute-start(bf16[528,1024]{1,0:T(8,128)(2,1)} %get-tuple-element.119), channel_id=1, source_target_pairs={{0,1},{1,0},{2,3},{3,2},{4,5},{5,4},{6,7},{7,6},{8,9},{9,8},{10,11... | collective-permute-start | bytes 3244040 | tf_op jit(solution)/shard_map/ppermute | solution.py:617
  3.9 18.4 %collective-permute-start.3 = (bf16[304,1024]{1,0:T(8,128)(2,1)}, bf16[304,1024]{1,0:T(8,128)(2,1)S(1)}, u32[]{:S(2)}, u32[]{:S(2)}) collective-permute-start(bf16[304,1024]{1,0:T(8,128)(2,1)} %get-tuple-element.122), channel_id=1, source_target_pairs={{1,2},{3,4},{5,6},{7,8},{9,10},{11,12},{13,14},{2,1},{4,3},{6,5},{... | collective-permute-start | bytes 1867784 | tf_op jit(solution)/shard_map/ppermute | solution.py:616
  7.7 14.7 %copy-start.5 = (f32[1024]{0:T(1024)S(1)}, f32[1024]{0:T(1024)}, u32[]{:S(2)}) copy-start(f32[1024]{0:T(1024)} %param.25) | copy-start | bytes 12292
  37.4 7.0 %copy-start = (f32[8,128]{1,0:T(8,128)S(1)}, f32[8,128]{1,0:T(8,128)}, u32[]{:S(2)}) copy-start(f32[8,128]{1,0:T(8,128)} %get-tuple-element.146.far_slots.refs_11_) | copy-start | bytes 12292
  37.4 7.0 %copy-start.1 = (f32[16,128]{1,0:T(8,128)S(1)}, f32[16,128]{1,0:T(8,128)}, u32[]{:S(2)}) copy-start(f32[16,128]{1,0:T(8,128)} %get-tuple-element.145.far_codes) | copy-start | bytes 24580
  38.0 6.4 %collective-permute-start.5 = (bf16[512,1024]{1,0:T(8,128)(2,1)}, bf16[512,1024]{1,0:T(8,128)(2,1)S(1)}, u32[]{:S(2)}, u32[]{:S(2)}) collective-permute-start(bf16[512,1024]{1,0:T(8,128)(2,1)} %get-tuple-element.142.cells_own.refs_2_), channel_id=1, source_target_pairs={{0,1},{1,0},{2,3},{3,2},{4,5},{5,4},{6,7},{7,6},{8,9},{9,8},{10,11... | collective-permute-start | bytes 3145736 | tf_op jit(solution)/shard_map/ppermute | solution.py:730
  38.1 13.5 %collective-permute-start.6 = (bf16[256,512]{1,0:T(8,128)(2,1)}, bf16[256,512]{1,0:T(8,128)(2,1)S(1)}, u32[]{:S(2)}, u32[]{:S(2)}) collective-permute-start(bf16[256,512]{1,0:T(8,128)(2,1)} %get-tuple-element.152), channel_id=1, source_target_pairs={{1,2},{3,4},{5,6},{7,8},{9,10},{11,12},{13,14},{2,1},{4,3},{6,5},{... | collective-permute-start | bytes 786440 | tf_op jit(solution)/shard_map/ppermute | solution.py:728
  40.7 14.2 %collective-permute-start.4 = (bf16[256,512]{1,0:T(8,128)(2,1)}, bf16[256,512]{1,0:T(8,128)(2,1)S(1)}, u32[]{:S(2)}, u32[]{:S(2)}) collective-permute-start(bf16[256,512]{1,0:T(8,128)(2,1)} %get-tuple-element.143), channel_id=1, source_target_pairs={{1,2},{3,4},{5,6},{7,8},{9,10},{11,12},{13,14},{2,1},{4,3},{6,5},{... | collective-permute-start | bytes 786440 | tf_op jit(solution)/shard_map/ppermute | solution.py:729
  44.4 7.2 %copy-start.2 = (bf16[512,1024]{1,0:T(8,128)(2,1)S(1)}, bf16[512,1024]{1,0:T(8,128)(2,1)}, u32[]{:S(2)}) copy-start(bf16[512,1024]{1,0:T(8,128)(2,1)} %get-tuple-element.142.cells_own.refs_2_) | copy-start | bytes 3145732

commit v3 on v2

--- a/solution.py
+++ b/solution.py
@@ -254,7 +254,7 @@
             else:
                 window = mid_b[last, at : at + 4 * lon, :]
                 own = mid_f[last, at + lon : at + 3 * lon, :]
-            value = (1.0 - c) * own + c * dot(mats[k][...], window)
+            value = own + c * (dot(mats[k][...], window) - own)
             k += 1
             if step < 3:
                 if half == 0:

time: 58.7 us -> 58.8 us (level)
  no operation moved by 1% of the time
where the time goes in v3:
time: 58.8 us; the launch traced here: 58.5 us
  Pallas kernels  38.5 us (65%)
  starting transfers between devices  9.42 us (16%)
  waiting for transfers between devices  8.05 us (14%)
  between operations  2.29 us (4%)
    pallas_call x1, Pallas kernels, run_observe(): pl.pallas_call(kernel, out_shape=column_shape + [pltpu.HBM((head, lon), F...  14.3 us
    pallas_call x1, Pallas kernels, run_near(): pl.pallas_call(near_kernel, out_shape=[slope_shape, slope_shape] + kept_s...  9.54 us
    pallas_call x2, Pallas kernels, finish(): pl.pallas_call(kernel, out_shape=shape((rows, lon, levels), F32), in_spec...  6.63 us
    ppermute x1, waiting for transfers between devices, local(): far = lax.ppermute(sent, 'lat', links)  5.11 us
    pallas_call x1, Pallas kernels, local(): pl.pallas_call(near_adjoint_kernel, out_shape=kept_shape + [shape((8, 2 *...  4.25 us
    ppermute x1, starting transfers between devices, local(): far_high = lax.ppermute(high, 'lat', links)  3.64 us
    pallas_call x1, Pallas kernels, local(): pl.pallas_call(pack_kernel, out_shape=[shape((cells + head, levels), BF16...  3.13 us
    ppermute x1, starting transfers between devices, local(): far = lax.ppermute(sent, 'lat', links)  3.05 us
  transfers between devices with their start and end apart: 5, of which 2 were waited for; matrix products, arithmetic and copies ran while one was open for 0% of the time, Pallas kernels for 29%

profile of v3, /device:TPU:25, one launch (start us, length us, event | category | flops | bytes accessed | tf_op | source)
XLA Modules:
  0.0 58.5 jit_solution(1297078643795546977)
XLA Ops:
  0.0 0.0 copy-start.3
  0.0 0.0 copy-start.4
  0.0 0.0 copy-start.6
  0.0 0.0 copy-start.7
  0.0 3.1 %pack.1 = (bf16[528,1024]{1,0:T(8,128)(2,1)}, bf16[304,1024]{1,0:T(8,128)(2,1)}, f32[16,128]{1,0:T(8,128)S(1)}, f32[8,128]{1,0:T(8,128)S(1)}) custom-call(s32[1]{0:T(128)} %bitcast.2.flip.refs_0_, f32[4,128,1024]{2,1,0:T(8,128)} %tangent.3, s32[4,4,128]{2,1,0:T(4,128)} %wind.1), custom_call_target="tpu_custom_call" | custom-call | tf_op jit(solution)/shard_map/pack/pallas_call | solution.py:597
  3.2 0.7 %collective-permute-start.2 = (bf16[528,1024]{1,0:T(8,128)(2,1)}, bf16[528,1024]{1,0:T(8,128)(2,1)}, u32[]{:S(2)}, u32[]{:S(2)}) collective-permute-start(bf16[528,1024]{1,0:T(8,128)(2,1)} %get-tuple-element.119), channel_id=1, source_target_pairs={{0,1},{1,0},{2,3},{3,2},{4,5},{5,4},{6,7},{7,6},{8,9},{9,8},{10,11... | collective-permute-start | bytes 3244040 | tf_op jit(solution)/shard_map/ppermute | solution.py:617
  3.9 3.0 %collective-permute-start.3 = (bf16[304,1024]{1,0:T(8,128)(2,1)}, bf16[304,1024]{1,0:T(8,128)(2,1)S(1)}, u32[]{:S(2)}, u32[]{:S(2)}) collective-permute-start(bf16[304,1024]{1,0:T(8,128)(2,1)} %get-tuple-element.122), channel_id=1, source_target_pairs={{1,2},{3,4},{5,6},{7,8},{9,10},{11,12},{13,14},{2,1},{4,3},{6,5},{... | collective-permute-start | bytes 1867784 | tf_op jit(solution)/shard_map/ppermute | solution.py:616
  7.6 0.0 collective-permute-done.2.near
  7.6 0.0 copy-done.3
  7.6 0.0 copy-done.4
  7.7 0.0 copy-done.6
  7.7 0.0 copy-done.7
  7.7 0.0 copy-start.5
  7.7 9.5 %near.3 = (f32[480,1024]{1,0:T(8,128)S(1)}, f32[480,1024]{1,0:T(8,128)S(1)}, f32[256,1024]{1,0:T(8,128)S(1)}, f32[256,1024]{1,0:T(8,128)S(1)}, f32[256,1024]{1,0...) custom-call(s32[1]{0:T(128)} %bitcast.2.flip.refs_0_, ...), custom_call_target="tpu_custom_call" | custom-call | flops 4000000000 | bytes 16000000 | tf_op jit(solution)/shard_map/near/pallas_call | solution.py:624
  17.2 5.1 %collective-permute-done.3.refs_6_ = bf16[304,1024]{1,0:T(8,128)(2,1)S(1)} collective-permute-done((bf16[304,1024]{1,0:T(8,128)(2,1)}, bf16[304,1024]{1,0:T(8,128)(2,1)S(1)}, u32[]{:S(2)}, u32[]{:S(2)}) %collective-permute-start.3) | collective-permute-done | bytes 622624 | tf_op jit(solution)/shard_map/ppermute | solution.py:616
  22.3 0.0 copy-done.5
  22.3 14.3 %observe.3 = (bf16[512,1024]{1,0:T(8,128)(2,1)}, bf16[256,512]{1,0:T(8,128)(2,1)}, bf16[256,512]{1,0:T(8,128)(2,1)}, f32[16,128]{1,0:T(8,128)}, f32[8,128]{1,0:T(8,128)}, /*index=5*/s32[1]{0:T(128)}, s32[1]{0:T(128)}) custom-call(s32[1]{0:T(128)} %bitcast.2.flip.refs_0_, s32[1]{0:T(128)} %bitcast.3.refs_1_, f32[8,128]{1,0:T(8,128)S(1)} %get-tuple-element.117.refs_2_, ...), custom_call_target="tpu_custom_call" | custom-call | tf_op jit(solution)/shard_map/observe/pallas_call | solution.py:673
  37.2 0.2 conditional.2
  37.5 0.0 copy-start
  37.5 0.0 copy-start.1
  37.5 0.6 %choose.1 = (bf16[512,1024]{1,0:T(8,128)(2,1)}, bf16[256,512]{1,0:T(8,128)(2,1)}, bf16[256,512]{1,0:T(8,128)(2,1)}) custom-call(s32[1]{0:T(128)} %get-tuple-element.135.flag, bf16[512,1024]{1,0:T(8,128)(2,1)} %get-tuple-element.136.refs_0_, bf16[256,512]{1,0:T(8,128)(2,1)} %get-tuple-element.137.refs_1_, ...), custom_call_target="tpu_custom_call", output_to_operand_aliasing={{0}: (1, {}), {1}: (2, {}), {2}: (3, {})} | custom-call | tf_op jit(solution)/shard_map/choose/pallas_call | solution.py:718
  38.1 0.1 collective-permute-start.5
  38.2 1.9 %collective-permute-start.6 = (bf16[256,512]{1,0:T(8,128)(2,1)}, bf16[256,512]{1,0:T(8,128)(2,1)S(1)}, u32[]{:S(2)}, u32[]{:S(2)}) collective-permute-start(bf16[256,512]{1,0:T(8,128)(2,1)} %get-tuple-element.152), channel_id=1, source_target_pairs={{1,2},{3,4},{5,6},{7,8},{9,10},{11,12},{13,14},{2,1},{4,3},{6,5},{... | collective-permute-start | bytes 786440 | tf_op jit(solution)/shard_map/ppermute | solution.py:728
  40.8 3.6 %collective-permute-start.4 = (bf16[256,512]{1,0:T(8,128)(2,1)}, bf16[256,512]{1,0:T(8,128)(2,1)S(1)}, u32[]{:S(2)}, u32[]{:S(2)}) collective-permute-start(bf16[256,512]{1,0:T(8,128)(2,1)} %get-tuple-element.143), channel_id=1, source_target_pairs={{1,2},{3,4},{5,6},{7,8},{9,10},{11,12},{13,14},{2,1},{4,3},{6,5},{... | collective-permute-start | bytes 786440 | tf_op jit(solution)/shard_map/ppermute | solution.py:729
  44.4 0.0 collective-permute-done.5.cells_near
  44.5 0.0 copy-done
  44.5 0.0 copy-done.1
  44.5 0.0 copy-start.2
  44.5 4.3 %near_adjoint.1 = (f32[256,1024]{1,0:T(8,128)S(1)}, f32[256,1024]{1,0:T(8,128)S(1)}, f32[256,1024]{1,0:T(8,128)S(1)}, bf16[8,256,512]{2,1,0:T(8,128)(2,1)S(1)}, bf16[512,256]{1,0:T(8,128)(2,1)S(1)}) custom-call(s32[1]{0:T(128)} %bitcast.2.flip.refs_0_, bf16[256,1024]{1,0:T(8,128)(2,1)} %get-tuple-element.160.rest.refs_4_, ...), custom_call_target="tpu_custom_call" | custom-call | flops 2000000000 | bytes 8000000 | tf_op jit(solution)/shard_map/near_adjoint/pallas_call | solution.py:738
  48.7 2.9 %collective-permute-done.6.refs_3_ = bf16[256,512]{1,0:T(8,128)(2,1)S(1)} collective-permute-done((bf16[256,512]{1,0:T(8,128)(2,1)}, bf16[256,512]{1,0:T(8,128)(2,1)S(1)}, u32[]{:S(2)}, u32[]{:S(2)}) %collective-permute-start.6) | collective-permute-done | bytes 262176 | tf_op jit(solution)/shard_map/ppermute | solution.py:728
  51.7 0.0 copy-done.2
  51.7 3.3 %far_adjoint.2.refs_12_ = f32[4,128,1024]{2,1,0:T(8,128)} custom-call(s32[1]{0:T(128)} %bitcast.2.flip.refs_0_, s32[1]{0:T(128)} %get-tuple-element.134.refs_1_, bf16[512,1024]{1,0:T(8,128)(2,1)S(1)} %copy-done.2, bf16[256,512]{1,0:T(8,128)(2,1)S(1)} %collective-permute-done.6.refs_3_, bf16[256,1024]{1,0:T(8,128)(2,1)} %get-tuple-element.160.rest.refs_4_, ...), custom_call_target="tpu_custom_call" | custom-call | flops 2000000000 | bytes 4000000 | tf_op jit(solution)/shard_map/far_adjoint/pallas_call | solution.py:774
  55.0 0.0 collective-permute-done.4.refs_3_
  55.0 3.3 %far_adjoint.3 = f32[4,128,1024]{2,1,0:T(8,128)} custom-call(s32[1]{0:T(128)} %bitcast.2.flip.refs_0_, s32[1]{0:T(128)} %get-tuple-element.134.refs_1_, bf16[512,1024]{1,0:T(8,128)(2,1)S(1)} %copy-done.2, bf16[256,512]{1,0:T(8,128)(2,1)S(1)} %collective-permute-done.4.refs_3_, ...), custom_call_target="tpu_custom_call", output_to_operand_aliasing={{}: (12, {})} | custom-call | flops 2000000000 | bytes 4000000 | tf_op jit(solution)/shard_map/far_adjoint/pallas_call | solution.py:774
  (3 shorter events, 0.0 us)
Async XLA Ops:
  0.0 7.6 %copy-start.3 = (f32[4,128,1024]{2,1,0:T(8,128)S(1)}, f32[4,128,1024]{2,1,0:T(8,128)}, u32[]{:S(2)}) copy-start(f32[4,128,1024]{2,1,0:T(8,128)} %tangent.3) | copy-start | bytes 6291460
  0.0 7.6 %copy-start.4 = (f32[1024]{0:T(1024)S(1)}, f32[1024]{0:T(1024)}, u32[]{:S(2)}) copy-start(f32[1024]{0:T(1024)} %param.17) | copy-start | bytes 12292
  0.0 7.6 %copy-start.6 = (s32[1,480]{1,0:T(1,128)S(1)}, s32[1,480]{1,0:T(1,128)}, u32[]{:S(2)}) copy-start(s32[1,480]{1,0:T(1,128)} %obs_index.1) | copy-start | bytes 5764
  0.0 7.7 %copy-start.7 = (bf16[1,480]{1,0:T(2,128)(2,1)S(1)}, bf16[1,480]{1,0:T(2,128)(2,1)}, u32[]{:S(2)}) copy-start(bf16[1,480]{1,0:T(2,128)(2,1)} %obs_quality.1) | copy-start | bytes 2884
  3.2 4.5 %collective-permute-start.2 = (bf16[528,1024]{1,0:T(8,128)(2,1)}, bf16[528,1024]{1,0:T(8,128)(2,1)}, u32[]{:S(2)}, u32[]{:S(2)}) collective-permute-start(bf16[528,1024]{1,0:T(8,128)(2,1)} %get-tuple-element.119), channel_id=1, source_target_pairs={{0,1},{1,0},{2,3},{3,2},{4,5},{5,4},{6,7},{7,6},{8,9},{9,8},{10,11... | collective-permute-start | bytes 3244040 | tf_op jit(solution)/shard_map/ppermute | solution.py:617
  3.9 18.4 %collective-permute-start.3 = (bf16[304,1024]{1,0:T(8,128)(2,1)}, bf16[304,1024]{1,0:T(8,128)(2,1)S(1)}, u32[]{:S(2)}, u32[]{:S(2)}) collective-permute-start(bf16[304,1024]{1,0:T(8,128)(2,1)} %get-tuple-element.122), channel_id=1, source_target_pairs={{1,2},{3,4},{5,6},{7,8},{9,10},{11,12},{13,14},{2,1},{4,3},{6,5},{... | collective-permute-start | bytes 1867784 | tf_op jit(solution)/shard_map/ppermute | solution.py:616
  7.7 14.7 %copy-start.5 = (f32[1024]{0:T(1024)S(1)}, f32[1024]{0:T(1024)}, u32[]{:S(2)}) copy-start(f32[1024]{0:T(1024)} %param.25) | copy-start | bytes 12292
  37.5 7.0 %copy-start = (f32[8,128]{1,0:T(8,128)S(1)}, f32[8,128]{1,0:T(8,128)}, u32[]{:S(2)}) copy-start(f32[8,128]{1,0:T(8,128)} %get-tuple-element.146.far_slots.refs_11_) | copy-start | bytes 12292
  37.5 7.0 %copy-start.1 = (f32[16,128]{1,0:T(8,128)S(1)}, f32[16,128]{1,0:T(8,128)}, u32[]{:S(2)}) copy-start(f32[16,128]{1,0:T(8,128)} %get-tuple-element.145.far_codes) | copy-start | bytes 24580
  38.1 6.4 %collective-permute-start.5 = (bf16[512,1024]{1,0:T(8,128)(2,1)}, bf16[512,1024]{1,0:T(8,128)(2,1)S(1)}, u32[]{:S(2)}, u32[]{:S(2)}) collective-permute-start(bf16[512,1024]{1,0:T(8,128)(2,1)} %get-tuple-element.142.cells_own.refs_2_), channel_id=1, source_target_pairs={{0,1},{1,0},{2,3},{3,2},{4,5},{5,4},{6,7},{7,6},{8,9},{9,8},{10,11... | collective-permute-start | bytes 3145736 | tf_op jit(solution)/shard_map/ppermute | solution.py:730
  38.2 13.5 %collective-permute-start.6 = (bf16[256,512]{1,0:T(8,128)(2,1)}, bf16[256,512]{1,0:T(8,128)(2,1)S(1)}, u32[]{:S(2)}, u32[]{:S(2)}) collective-permute-start(bf16[256,512]{1,0:T(8,128)(2,1)} %get-tuple-element.152), channel_id=1, source_target_pairs={{1,2},{3,4},{5,6},{7,8},{9,10},{11,12},{13,14},{2,1},{4,3},{6,5},{... | collective-permute-start | bytes 786440 | tf_op jit(solution)/shard_map/ppermute | solution.py:728
  40.8 14.3 %collective-permute-start.4 = (bf16[256,512]{1,0:T(8,128)(2,1)}, bf16[256,512]{1,0:T(8,128)(2,1)S(1)}, u32[]{:S(2)}, u32[]{:S(2)}) collective-permute-start(bf16[256,512]{1,0:T(8,128)(2,1)} %get-tuple-element.143), channel_id=1, source_target_pairs={{1,2},{3,4},{5,6},{7,8},{9,10},{11,12},{13,14},{2,1},{4,3},{6,5},{... | collective-permute-start | bytes 786440 | tf_op jit(solution)/shard_map/ppermute | solution.py:729
  44.5 7.2 %copy-start.2 = (bf16[512,1024]{1,0:T(8,128)(2,1)S(1)}, bf16[512,1024]{1,0:T(8,128)(2,1)}, u32[]{:S(2)}) copy-start(bf16[512,1024]{1,0:T(8,128)(2,1)} %get-tuple-element.142.cells_own.refs_2_) | copy-start | bytes 3145732
